TPU v7x, 32 devices: a whole 2x2x4 slice. The times are simulated.
32 devices in a mesh: day: 2 (over y), chan: 16 (over z, x, core).
Axes of the slice: x: 2, y: 2, z: 4, core: 2. Of those that a mesh axis runs over, the one named last changes fastest.
Arguments:
- traces: bfloat16 [2560, 16, 1500], P(('day', 'chan')), parts along dimension 0, may hold values from -6 to 6
- quality: int32 [2560, 16], P(('day', 'chan')), parts along dimension 0, may hold values 0 or 1
- reach: int32 [2560], P(('day', 'chan')), parts along dimension 0, may hold values from 0 to 160
Outputs:
- correlations: bfloat16 [2560, 161, 201], P(('day', 'chan')), parts along dimension 0
There are 2 independent parts, one for each index of `day`. A program takes and returns all parts, laid end to end along the dimension named above; each array names one. Nothing has to cross between parts.
All inputs are finite; a program needn't handle non-finite values. No bound on the sum of `quality` on one device may be relied on, other than what follows from the above.
Results may differ from a plain program's by a relative error of at most 0.0059.
Values may be sent and summed in bfloat16 or wider, within the bound.
A program may use at most 128 MiB of HBM per device.

v0:
```python
import math

import jax
import jax.numpy as jnp
from jax import lax
from jax.sharding import PartitionSpec as P

R = 160
S = 1500
F = 256
HALF_SMOOTH = 32
LARGEST_LAG_SPAN = 100
FREQ_BLOCK = 128


eps = 1e-06


def from_behind(value, axis, steps):
    count = lax.axis_size(axis)
    initial, last = (max(0, -steps), min(count, count - steps))
    return lax.ppermute(value, axis, [(source, source + steps) for source in range(initial, last)])


def dft_table():
    times = jnp.arange(S, dtype=jnp.int32)
    bins = 1 + jnp.arange(F + 2 * HALF_SMOOTH, dtype=jnp.int32)
    phase = times[:, None] * bins[None, :] % S
    angle = 2.0 * math.pi / S * phase.astype(jnp.float32)
    return jnp.concatenate([jnp.cos(angle), -jnp.sin(angle)], axis=1).astype(jnp.bfloat16)


def smoothing_table():
    inner = jnp.arange(F + 2 * HALF_SMOOTH, dtype=jnp.int32)[:, None]
    outer = jnp.arange(F, dtype=jnp.int32)[None, :]
    return ((inner >= outer) & (inner <= outer + 2 * HALF_SMOOTH)).astype(jnp.float32)


def lag_table():
    bins = 1 + HALF_SMOOTH + jnp.arange(F, dtype=jnp.int32)
    shifts = jnp.arange(2 * LARGEST_LAG_SPAN + 1, dtype=jnp.int32) - LARGEST_LAG_SPAN
    phase = bins[:, None] * shifts[None, :] % S
    angle = 2.0 * math.pi / S * phase.astype(jnp.float32)
    return jnp.concatenate([jnp.cos(angle), -jnp.sin(angle)], axis=0).astype(jnp.bfloat16)


def whiten_masked(masked):
    count, window_segments, samples = masked.shape
    spectra = jnp.dot(
        masked.reshape(count * window_segments, samples),
        dft_table(),
        preferred_element_type=jnp.float32,
    )
    half = spectra.shape[1] // 2
    real_component = spectra[:, :half]
    imag_part = spectra[:, half:]
    amplitude = jnp.sqrt(real_component * real_component + imag_part * imag_part)
    smooth = jnp.dot(amplitude, smoothing_table(), precision=lax.Precision.HIGHEST) / (
        2 * HALF_SMOOTH + 1
    )
    scale = 1.0 / (smooth + eps)
    core = jnp.concatenate(
        [
            real_component[:, HALF_SMOOTH : HALF_SMOOTH + F] * scale,
            imag_part[:, HALF_SMOOTH : HALF_SMOOTH + F] * scale,
        ],
        axis=1,
    )
    return core.astype(jnp.bfloat16).reshape(count, window_segments, 2 * F)


def diagonals(launch_lattice):
    blocks, rows, cols = launch_lattice.shape
    flat = launch_lattice.reshape(blocks, rows * cols)
    flat = jnp.concatenate([flat, jnp.zeros((blocks, rows), jnp.float32)], axis=1)
    return flat.reshape(blocks, rows, cols + 1)[:, :, : R + 1]


def batched_gram(left_part, right_part):
    numbers = (((1,), (1,)), ((0,), (0,)))
    return lax.dot_general(left_part, right_part, numbers, preferred_element_type=jnp.float32)


def correlate(frequency_major, reach_part):
    two_f, window_segments, span = frequency_major.shape
    chans = span - R
    lag_all = lag_table()

    def one_block(total, index):
        start = index * FREQ_BLOCK
        ext_real = lax.dynamic_slice_in_dim(frequency_major, start, FREQ_BLOCK, 0)
        ext_imag = lax.dynamic_slice_in_dim(frequency_major, F + start, FREQ_BLOCK, 0)
        left_real = ext_real[:, :, :chans]
        left_imag = ext_imag[:, :, :chans]
        real_sum = (
            batched_gram(left_real, ext_real) + batched_gram(left_imag, ext_imag)
        ) / window_segments
        imag_sum = (
            batched_gram(left_imag, ext_real) - batched_gram(left_real, ext_imag)
        ) / window_segments
        cross = jnp.concatenate([diagonals(real_sum), diagonals(imag_sum)], axis=0).astype(
            jnp.bfloat16
        )
        rows = jnp.concatenate(
            [
                lax.dynamic_slice_in_dim(lag_all, start, FREQ_BLOCK, 0),
                lax.dynamic_slice_in_dim(lag_all, F + start, FREQ_BLOCK, 0),
            ],
            axis=0,
        )
        lagged = lax.dot_general(
            cross, rows, (((0,), (0,)), ((), ())), preferred_element_type=jnp.float32
        )
        return (total + lagged, None)

    starting_carry = jnp.zeros((chans, R + 1, 2 * LARGEST_LAG_SPAN + 1), jnp.float32)
    total, _ = lax.scan(one_block, starting_carry, jnp.arange(F // FREQ_BLOCK, dtype=jnp.int32))
    offsets = jnp.arange(R + 1, dtype=jnp.int32)
    keep = offsets[None, :] <= reach_part[:, None]
    return jnp.where(keep[:, :, None], total / math.sqrt(F), 0.0).astype(jnp.bfloat16)


def gather_upcoming_traces(block):
    nearer = from_behind(block, "chan", -1)
    farther = from_behind(block, "chan", -2)
    return (nearer, farther)


def local(traces, quality, reach):
    chans = traces.shape[0]
    span = chans + R
    masked = traces * quality[:, :, None].astype(jnp.bfloat16)
    nearer, farther = gather_upcoming_traces(masked)
    extended = whiten_masked(jnp.concatenate([masked, nearer, farther], axis=0))
    frequency_major = jnp.transpose(extended, (2, 1, 0))
    return correlate(frequency_major, reach)


def solution(mesh):
    return jax.shard_map(
        local,
        mesh=mesh,
        in_specs=(P(("day", "chan"), None, None), P(("day", "chan"), None), P(("day", "chan"))),
        out_specs=P(("day", "chan"), None, None),
        check_vma=False,
    )
```

profile of v0, /device:TPU:0, one launch (start us, length us, event | category | flops | bytes accessed | tf_op | source)
XLA Modules:
  0.0 350.8 jit_solution(9879370427623027748)
XLA Ops:
  0.0 0.7 convert_element_type.26
  0.7 0.1 copy.12
  0.8 4.4 %broadcast_multiply_fusion = bf16[80,16,1500]{2,1,0:T(8,128)(2,1)} fusion(bf16[80,16,1500]{2,1,0:T(8,128)(2,1)} %param.5, bf16[80,16]{1,0:T(8,128)(2,1)S(1)} %copy.12), kind=kLoop, calls=%fused_computation.52 | loop fusion | flops 1920000 | bytes 7682560 | tf_op jit(solution)/shard_map/mul | solution.py:132
  5.2 1.3 collective-permute-start
  6.5 1.3 collective-permute-start.1
  7.8 1.1 cosine_convert_fusion.1
  8.9 0.7 pad_maximum_fusion.1
  9.6 0.6 iota_compare_fusion.3
  10.2 9.9 %cosine_convert_fusion = (bf16[1500,320]{1,0:T(8,128)(2,1)S(1)}, bf16[1500,320]{1,0:T(8,128)(2,1)S(1)}) fusion(s32[320]{0:T(512)S(1)} %iota_add_fusion), kind=kLoop, calls=%fused_computation.47 | loop fusion | flops 5760000 | bytes 1921280 | tf_op jit(solution)/shard_map/convert.18
  20.1 0.0 collective-permute-done
  20.1 118.2 %collective-permute-done.1 = bf16[80,16,1500]{2,1,0:T(8,128)(2,1)} collective-permute-done((bf16[80,16,1500]{2,1,0:T(8,128)(2,1)}, bf16[80,16,1500]{2,1,0:T(8,128)(2,1)}, u32[]{:S(2)}, u32[]{:S(2)}) %collective-permute-start.1) | collective-permute-done | bytes 3840032 | tf_op jit(solution)/shard_map/ppermute | solution.py:22
  138.3 6.7 %pad_maximum_fusion = bf16[240,16,1500]{2,1,0:T(8,128)(2,1)S(1)} fusion(bf16[80,16,1500]{2,1,0:T(8,128)(2,1)} %collective-permute-done.1, bf16[80,16,1500]{2,1,0:T(8,128)(2,1)} %collective-permute-done, bf16[80,16,1500]{2,1,0:T(8,128)(2,1)} %broadcast_multiply_fusion), kind=kLoop, calls=%fused_computation.29 | loop fusion | flops 11520000 | bytes 23040000 | tf_op jit(solution)/shard_map/concatenate | solution.py:134
  145.0 10.0 %fusion.42 = f32[3840,640]{1,0:T(8,128)S(1)} fusion(bf16[3840,1500]{1,0:T(8,128)(2,1)S(1)} %bitcast.26, bf16[1500,320]{1,0:T(8,128)(2,1)S(1)} %get-tuple-element.106, bf16[1500,320]{1,0:T(8,128)(2,1)S(1)} %get-tuple-element.105), kind=kOutput, calls=%fused_computation.53 | convolution fusion | flops 7376640000 | bytes 23270400 | tf_op jit(solution)/shard_map/dot_general | solution.py:49
  154.9 7.9 %fusion.33 = (bf16[3840,256]{1,0:T(8,128)(2,1)}, bf16[3840,256]{1,0:T(8,128)(2,1)}) fusion(f32[3840,640]{1,0:T(8,128)S(1)} %fusion.42, s32[256]{0:T(256)S(1)} %iota_add_fusion.3), kind=kOutput, calls=%fused_computation.41 | convolution fusion | flops 3785687040 | bytes 23593984 | tf_op jit(solution)/shard_map/dot_general | solution.py:58
  162.9 3.8 %copy.13 = bf16[240,16,256]{0,1,2:T(8,128)(2,1)S(1)} copy(bf16[240,16,256]{2,1,0:T(8,128)(2,1)} %bitcast.28) | data formatting | bytes 3932160 | tf_op jit(solution)/shard_map/concatenate | solution.py:62
  166.7 4.8 %copy.14 = bf16[240,16,256]{0,1,2:T(8,128)(2,1)} copy(bf16[240,16,256]{2,1,0:T(8,128)(2,1)} %bitcast.27) | data formatting | bytes 3932160 | tf_op jit(solution)/shard_map/concatenate | solution.py:62
  171.5 4.2 %maximum_bitcast_fusion.2 = bf16[512,16,240]{2,1,0:T(8,128)(2,1)} fusion(bf16[240,16,256]{0,1,2:T(8,128)(2,1)} %copy.14, bf16[240,16,256]{0,1,2:T(8,128)(2,1)S(1)} %copy.13), kind=kLoop, calls=%fused_computation.37 | loop fusion | flops 1966080 | bytes 7864320 | tf_op jit(solution)/shard_map/transpose | solution.py:135
  175.7 163.3 %while.13 = (s32[]{:T(128)}, f32[80,161,201]{2,1,0:T(8,128)}, s32[2]{0:T(128)S(1)}, bf16[512,16,240]{2,1,0:T(8,128)(2,1)}, bf16[512,201]{0,1:T(8,128)(2,1)}, /*i...) while((s32[]{:T(128)}, f32[80,161,201]{2,1,0:T(8,128)}, ...), condition=%wide.region_1.2_spmd.clone, body=%wide.region_0.1_spmd.clone.sunk | while | flops 1673397760 | bytes 176801232 | solution.py:117
  175.7 0.6 dynamic_slice.57
  177.0 6.8 %fusion.77 = f32[128,80,240]{2,1,0:T(8,128)} fusion(bf16[512,16,240]{2,1,0:T(8,128)(2,1)} %get-tuple-element.169, s32[]{:T(128)S(6)} %select_n.63), kind=kOutput, calls=%fused_computation.8.clone.1 | convolution fusion | flops 78643200 | bytes 11404288 | tf_op jit(solution)/shard_map/while/body/eval_jaxpr/dot_general | solution.py:81
  183.8 8.4 %multiply_convert_fusion.5 = bf16[128,80,240]{2,1,0:T(8,128)(2,1)} fusion(f32[128,80,240]{2,1,0:T(8,128)} %fusion.77, bf16[512,16,240]{2,1,0:T(8,128)(2,1)} %get-tuple-element.169, s32[]{:T(128)S(6)} %select_n.64), kind=kOutput, calls=%fused_computation.2.clone.1 | convolution fusion | flops 86016000 | bytes 16974848 | tf_op jit(solution)/shard_map/while/body/eval_jaxpr/dot_general | solution.py:81
  192.2 8.7 %copy.24 = bf16[128,80,240]{0,2,1:T(8,128)(2,1)} copy(bf16[128,80,240]{2,1,0:T(8,128)(2,1)} %multiply_convert_fusion.5) | data formatting | bytes 9830400 | tf_op jit(solution)/shard_map/convert.11
  201.0 5.5 %concatenate.52 = bf16[128,19280]{0,1:T(8,128)(2,1)} pad(bf16[128,19200]{0,1:T(8,128)(2,1)} %bitcast.25, bf16[]{:T(256)} %constant.79.clone.2..sunk), padding=0_0x0_80 | pad | bytes 9850882 | tf_op jit(solution)/shard_map/while/body/eval_jaxpr/concatenate | solution.py:75
  206.5 6.9 %reshape.87 = bf16[128,80,241]{0,2,1:T(8,128)(2,1)} reshape(bf16[128,19280]{0,1:T(8,128)(2,1)} %concatenate.52) | data formatting | bytes 9871360 | tf_op jit(solution)/shard_map/while/body/eval_jaxpr/reshape | solution.py:76
  213.4 2.2 copy-done
  215.6 1.6 fusion.76
  217.2 3.9 %multiply_convert_fusion.4 = bf16[128,80,240]{2,1,0:T(8,128)(2,1)} fusion(f32[128,80,240]{2,1,0:T(8,128)S(1)} %fusion.76, bf16[512,16,240]{2,1,0:T(8,128)(2,1)S(1)} %copy-done, s32[]{:T(128)S(6)} %select_n.64, s32[]{:T(128)S(6)} %select_n.63), kind=kOutput, calls=%fused_computation.1.clone.1 | convolution fusion | flops 86016000 | bytes 16973832 | tf_op jit(solution)/shard_map/while/body/eval_jaxpr/dot_general | solution.py:81
  221.1 8.6 %copy.23 = bf16[128,80,240]{0,2,1:T(8,128)(2,1)} copy(bf16[128,80,240]{2,1,0:T(8,128)(2,1)} %multiply_convert_fusion.4) | data formatting | bytes 9830400 | tf_op jit(solution)/shard_map/convert.6
  229.8 5.6 %concatenate.51 = bf16[128,19280]{0,1:T(8,128)(2,1)} pad(bf16[128,19200]{0,1:T(8,128)(2,1)} %bitcast.24, bf16[]{:T(256)} %constant.79.clone.2..sunk), padding=0_0x0_80 | pad | bytes 9850882 | tf_op jit(solution)/shard_map/while/body/eval_jaxpr/concatenate | solution.py:75
  235.4 6.9 %reshape.86 = bf16[128,80,241]{0,2,1:T(8,128)(2,1)} reshape(bf16[128,19280]{0,1:T(8,128)(2,1)} %concatenate.51) | data formatting | bytes 9871360 | tf_op jit(solution)/shard_map/while/body/eval_jaxpr/reshape | solution.py:76
  242.3 4.2 %slice.88 = bf16[128,80,161]{0,2,1:T(8,128)(2,1)} slice(bf16[128,80,241]{0,2,1:T(8,128)(2,1)} %reshape.86), slice={[0:128], [0:80], [0:161]} | slice | bytes 6594560 | tf_op jit(solution)/shard_map/while/body/eval_jaxpr/slice | solution.py:76
  246.4 0.0 copy-done.1
  246.5 8.9 %select_add_fusion.2 = f32[80,161,201]{2,1,0:T(8,128)} fusion(f32[80,161,201]{2,1,0:T(8,128)} %get-tuple-element.155, bf16[128,80,161]{0,2,1:T(8,128)(2,1)} %slice.88, bf16[128,80,161]{0,2,1:T(8,128)(2,1)S(1)} %slice-done, pred[]{:T(512)S(6)} %compare.5, bf16[128,201]{0,1:T(8,128)(2,1)S(1)} %get-tuple-element.140, ...), kind=kOutput, calls=%fused_computation.clone.1 | convolution fusion | flops 1344079360 | bytes 27408512 | tf_op jit(solution)/shard_map/while/body/eval_jaxpr/dot_general | solution.py:111
  255.4 0.6 dynamic_slice.57
  256.6 6.8 %fusion.77 = f32[128,80,240]{2,1,0:T(8,128)} fusion(bf16[512,16,240]{2,1,0:T(8,128)(2,1)} %get-tuple-element.169, s32[]{:T(128)S(6)} %select_n.63), kind=kOutput, calls=%fused_computation.8.clone.1 | convolution fusion | flops 78643200 | bytes 11404288 | tf_op jit(solution)/shard_map/while/body/eval_jaxpr/dot_general | solution.py:81
  263.5 8.4 %multiply_convert_fusion.5 = bf16[128,80,240]{2,1,0:T(8,128)(2,1)} fusion(f32[128,80,240]{2,1,0:T(8,128)} %fusion.77, bf16[512,16,240]{2,1,0:T(8,128)(2,1)} %get-tuple-element.169, s32[]{:T(128)S(6)} %select_n.64), kind=kOutput, calls=%fused_computation.2.clone.1 | convolution fusion | flops 86016000 | bytes 16974848 | tf_op jit(solution)/shard_map/while/body/eval_jaxpr/dot_general | solution.py:81
  271.9 8.7 %copy.24 = bf16[128,80,240]{0,2,1:T(8,128)(2,1)} copy(bf16[128,80,240]{2,1,0:T(8,128)(2,1)} %multiply_convert_fusion.5) | data formatting | bytes 9830400 | tf_op jit(solution)/shard_map/convert.11
  280.6 5.5 %concatenate.52 = bf16[128,19280]{0,1:T(8,128)(2,1)} pad(bf16[128,19200]{0,1:T(8,128)(2,1)} %bitcast.25, bf16[]{:T(256)} %constant.79.clone.2..sunk), padding=0_0x0_80 | pad | bytes 9850882 | tf_op jit(solution)/shard_map/while/body/eval_jaxpr/concatenate | solution.py:75
  286.2 6.9 %reshape.87 = bf16[128,80,241]{0,2,1:T(8,128)(2,1)} reshape(bf16[128,19280]{0,1:T(8,128)(2,1)} %concatenate.52) | data formatting | bytes 9871360 | tf_op jit(solution)/shard_map/while/body/eval_jaxpr/reshape | solution.py:76
  293.1 2.2 copy-done
  295.3 1.6 fusion.76
  296.9 3.9 %multiply_convert_fusion.4 = bf16[128,80,240]{2,1,0:T(8,128)(2,1)} fusion(f32[128,80,240]{2,1,0:T(8,128)S(1)} %fusion.76, bf16[512,16,240]{2,1,0:T(8,128)(2,1)S(1)} %copy-done, s32[]{:T(128)S(6)} %select_n.64, s32[]{:T(128)S(6)} %select_n.63), kind=kOutput, calls=%fused_computation.1.clone.1 | convolution fusion | flops 86016000 | bytes 16973832 | tf_op jit(solution)/shard_map/while/body/eval_jaxpr/dot_general | solution.py:81
  300.8 8.6 %copy.23 = bf16[128,80,240]{0,2,1:T(8,128)(2,1)} copy(bf16[128,80,240]{2,1,0:T(8,128)(2,1)} %multiply_convert_fusion.4) | data formatting | bytes 9830400 | tf_op jit(solution)/shard_map/convert.6
  309.4 5.6 %concatenate.51 = bf16[128,19280]{0,1:T(8,128)(2,1)} pad(bf16[128,19200]{0,1:T(8,128)(2,1)} %bitcast.24, bf16[]{:T(256)} %constant.79.clone.2..sunk), padding=0_0x0_80 | pad | bytes 9850882 | tf_op jit(solution)/shard_map/while/body/eval_jaxpr/concatenate | solution.py:75
  315.0 6.9 %reshape.86 = bf16[128,80,241]{0,2,1:T(8,128)(2,1)} reshape(bf16[128,19280]{0,1:T(8,128)(2,1)} %concatenate.51) | data formatting | bytes 9871360 | tf_op jit(solution)/shard_map/while/body/eval_jaxpr/reshape | solution.py:76
  321.9 4.2 %slice.88 = bf16[128,80,161]{0,2,1:T(8,128)(2,1)} slice(bf16[128,80,241]{0,2,1:T(8,128)(2,1)} %reshape.86), slice={[0:128], [0:80], [0:161]} | slice | bytes 6594560 | tf_op jit(solution)/shard_map/while/body/eval_jaxpr/slice | solution.py:76
  326.1 12.9 %select_add_fusion.2 = f32[80,161,201]{2,1,0:T(8,128)} fusion(f32[80,161,201]{2,1,0:T(8,128)} %get-tuple-element.155, bf16[128,80,161]{0,2,1:T(8,128)(2,1)} %slice.88, bf16[128,80,161]{0,2,1:T(8,128)(2,1)S(1)} %slice-done, pred[]{:T(512)S(6)} %compare.5, bf16[128,201]{0,1:T(8,128)(2,1)S(1)} %get-tuple-element.140, ...), kind=kOutput, calls=%fused_computation.clone.1 | convolution fusion | flops 1344079360 | bytes 27408512 | tf_op jit(solution)/shard_map/while/body/eval_jaxpr/dot_general | solution.py:111
  339.0 11.7 %fusion.21 = bf16[80,161,201]{2,0,1:T(8,128)(2,1)} fusion(f32[80,161,201]{2,1,0:T(8,128)} %get-tuple-element.70, pred[80,161]{0,1:T(8,128)(4,1)} %iota_compare_fusion.3), kind=kLoop, calls=%fused_computation.28 | loop fusion | flops 7766640 | bytes 15546160 | tf_op jit(solution)/shard_map/convert_element_type | solution.py:120
  (19 shorter events, 0.1 us)
Async XLA Ops:
  0.8 8.8 %copy-start.2 = (s32[80]{0:T(128)S(1)}, s32[80]{0:T(128)}, u32[]{:S(2)}) copy-start(s32[80]{0:T(128)} %param.7) | copy-start | bytes 964
  5.2 14.9 %collective-permute-start = (bf16[80,16,1500]{2,1,0:T(8,128)(2,1)}, bf16[80,16,1500]{2,1,0:T(8,128)(2,1)}, u32[]{:S(2)}, u32[]{:S(2)}) collective-permute-start(bf16[80,16,1500]{2,1,0:T(8,128)(2,1)} %broadcast_multiply_fusion), channel_id=1, source_target_pairs={{1,0},{2,1},{3,2},{4,3},{5,4},{6,5},{7,6},{8,7},{9,8},{10,9},{11,1... | collective-permute-start | bytes 11520008 | tf_op jit(solution)/shard_map/ppermute | solution.py:22
  6.5 131.8 %collective-permute-start.1 = (bf16[80,16,1500]{2,1,0:T(8,128)(2,1)}, bf16[80,16,1500]{2,1,0:T(8,128)(2,1)}, u32[]{:S(2)}, u32[]{:S(2)}) collective-permute-start(bf16[80,16,1500]{2,1,0:T(8,128)(2,1)} %broadcast_multiply_fusion), channel_id=1, source_target_pairs={{2,0},{3,1},{4,2},{5,3},{6,4},{7,5},{8,6},{9,7},{10,8},{11,9},{12,... | collective-permute-start | bytes 11520008 | tf_op jit(solution)/shard_map/ppermute | solution.py:22
  213.4 2.2 copy-start
  242.3 4.2 %copy-start.1 = (bf16[512,201]{0,1:T(8,128)(2,1)S(1)}, bf16[512,201]{0,1:T(8,128)(2,1)}, u32[]{:S(2)}) copy-start(bf16[512,201]{0,1:T(8,128)(2,1)} %get-tuple-element.170) | copy-start | bytes 617476 | tf_op jit(solution)/shard_map/while
  242.3 4.2 %slice-start = ((bf16[128,80,241]{0,2,1:T(8,128)(2,1)}), bf16[128,80,161]{0,2,1:T(8,128)(2,1)S(1)}, s32[]{:S(2)}) async-start(bf16[128,80,241]{0,2,1:T(8,128)(2,1)} %reshape.87), calls=%async_computation | async-start | bytes 6881280 | tf_op jit(solution)/shard_map/while/body/eval_jaxpr/slice | solution.py:76
  293.1 2.2 copy-start
  321.9 4.2 %copy-start.1 = (bf16[512,201]{0,1:T(8,128)(2,1)S(1)}, bf16[512,201]{0,1:T(8,128)(2,1)}, u32[]{:S(2)}) copy-start(bf16[512,201]{0,1:T(8,128)(2,1)} %get-tuple-element.170) | copy-start | bytes 617476 | tf_op jit(solution)/shard_map/while
  321.9 4.2 %slice-start = ((bf16[128,80,241]{0,2,1:T(8,128)(2,1)}), bf16[128,80,161]{0,2,1:T(8,128)(2,1)S(1)}, s32[]{:S(2)}) async-start(bf16[128,80,241]{0,2,1:T(8,128)(2,1)} %reshape.87), calls=%async_computation | async-start | bytes 6881280 | tf_op jit(solution)/shard_map/while/body/eval_jaxpr/slice | solution.py:76
where the time goes:
time: 353 us; the launch traced here: 351 us
  waiting for transfers between devices  118 us (33%)
  local copies, waits for them, and re-layouts  107 us (30%)
  matrix products  81.2 us (23%)
  other arithmetic  40 us (11%)
    ppermute x2, waiting for transfers between devices, from_behind(): lax.ppermute(value, axis, [(source, source + steps) for source in range(i...  118 us
    dot_general x8, matrix products, batched_gram(): lax.dot_general(left_part, right_part, numbers, preferred_element_type=jn...  41.5 us
    another operation x4, local copies, waits for them, and re-layouts  34.7 us
    reshape x4, local copies, waits for them, and re-layouts, diagonals(): return flat.reshape(blocks, rows, cols + 1)[:, :, :R + 1]  27.7 us
    concatenate x4, local copies, waits for them, and re-layouts, diagonals(): jnp.concatenate([flat, jnp.zeros((blocks, rows), jnp.float32)], axis=1)  22.3 us
    dot_general x2, matrix products, one_block(): lax.dot_general(cross, rows, (((0,), (0,)), ((), ())), preferred_element_...  21.8 us
    convert_element_type x1, other arithmetic, correlate(): jnp.where(keep[:, :, None], total / math.sqrt(F), 0.0).astype(jnp.bfloat16)  11.7 us
    another operation x2, other arithmetic  10.9 us
  transfers between devices with their start and end apart: 2, of which 1 were waited for; matrix products, arithmetic and copies ran while one was open for 3% of the time, Pallas kernels for 0%

commit v1 on v0

v1 whole, which is shorter than its diff:
```python
import math

import jax
import jax.numpy as jnp
import numpy as np
from jax import lax
from jax.experimental import pallas as pl
from jax.experimental.pallas import tpu as pltpu
from jax.sharding import PartitionSpec as P

R = 160
S = 1500
F = 256
HALF_SMOOTH = 32
BINS = F + 2 * HALF_SMOOTH
LAG = 100
LAGS = 2 * LAG + 1
LANES = 128
PIECES = -(-S // LANES)
GROUP = 8
GROUPS = F // GROUP
BAND = 176
SPAN = 256
STEP_GROUPS = 4
STEP_CHANS = 8
VMEM_LIMIT = 56 * 1024 * 1024

eps = 1e-06


def dft_rows():
    times = np.arange(S, dtype=np.int32)
    bins = 1 + np.arange(BINS, dtype=np.int32)
    phase = bins[:, None] * times[None, :] % S
    angle = np.float32(2.0 * math.pi / S) * phase.astype(np.float32)
    table = np.concatenate([np.cos(angle), -np.sin(angle)], axis=0)
    return np.pad(table, ((0, 0), (0, PIECES * LANES - S))).astype(jnp.bfloat16)


def band_rows():
    outer = np.arange(F)[:, None]
    inner = np.arange(BINS)[None, :]
    return ((inner >= outer) & (inner <= outer + 2 * HALF_SMOOTH)).astype(jnp.bfloat16)


def lag_rows(windows):
    bins = 1 + HALF_SMOOTH + np.arange(F, dtype=np.int32)
    shifts = np.arange(LAGS, dtype=np.int32) - LAG
    phase = shifts[:, None] * bins[None, :] % S
    angle = np.float32(2.0 * math.pi / S) * phase.astype(np.float32)
    both = np.stack([np.cos(angle), -np.sin(angle)], axis=1).astype(jnp.bfloat16)
    both = both.reshape(LAGS, 2, GROUPS, GROUP).transpose(0, 2, 1, 3).reshape(LAGS, 2 * F)
    scale = np.float32(1.0 / (windows * math.sqrt(F)))
    both = (both.astype(np.float32) * scale).astype(jnp.bfloat16)
    return np.concatenate([both, np.zeros((256 - LAGS, 2 * F), jnp.bfloat16)], axis=0)


def whiten_kernel(traces_ref, quality_ref, dft_ref, band_ref, out_ref, wide, turned):
    chans, windows, _ = traces_ref.shape
    pieces = wide.shape[0]
    for c in range(0, chans, 8):
        rows = traces_ref[c : c + 8].astype(jnp.float32).reshape(8 * windows, S)
        for p in range(pieces):
            piece = rows[:, p * LANES : (p + 1) * LANES]
            if piece.shape[1] < LANES:
                rest = jnp.zeros((8 * windows, LANES - piece.shape[1]), jnp.float32)
                piece = jnp.concatenate([piece, rest], axis=1)
            wide[p, c * windows : (c + 8) * windows, :] = piece
    fill = jnp.zeros((LANES - chans, pieces * LANES), jnp.bfloat16)

    def window(w):
        rows = [wide[p, pl.ds(w, chans, stride=windows), :] for p in range(pieces)]
        return jnp.concatenate(rows, axis=1).astype(jnp.bfloat16)

    for w in range(0, windows, 2):
        both = jnp.concatenate([window(w), fill, window(w + 1), fill], axis=0)
        spectra = lax.dot_general(
            dft_ref[...], both, (((1,), (1,)), ((), ())), preferred_element_type=jnp.float32
        )
        real = spectra[:BINS]
        imag = spectra[BINS:]
        amplitude = jnp.sqrt(real * real + imag * imag)
        high = amplitude.astype(jnp.bfloat16)
        low = (amplitude - high.astype(jnp.float32)).astype(jnp.bfloat16)
        smooth = jnp.dot(band_ref[...], high, preferred_element_type=jnp.float32)
        smooth = smooth + jnp.dot(band_ref[...], low, preferred_element_type=jnp.float32)
        scale = 1.0 / (smooth * (1.0 / (2 * HALF_SMOOTH + 1)) + eps)
        usable = quality_ref[:, w * LANES : (w + 2) * LANES]
        scale = scale * usable
        real = real[HALF_SMOOTH : HALF_SMOOTH + F] * scale
        imag = imag[HALF_SMOOTH : HALF_SMOOTH + F] * scale
        for j in range(2):
            lanes = slice(j * LANES, (j + 1) * LANES)
            turned[:, 0, w + j] = real[:, lanes].reshape(GROUPS, GROUP, LANES)
            turned[:, 1, w + j] = imag[:, lanes].reshape(GROUPS, GROUP, LANES)
    depth = 2 * windows * GROUP
    for g in range(GROUPS):
        block = turned[g].reshape(depth, LANES).T
        out_ref[:, g * depth : (g + 1) * depth] = block[:chans].astype(jnp.bfloat16)


def whiten(traces, quality):
    chans, windows, _ = traces.shape
    usable = jnp.pad(quality.astype(jnp.float32).T, ((0, 0), (0, LANES - chans)))
    usable = usable.reshape(1, windows * LANES)
    depth = 2 * windows * GROUP
    return pl.pallas_call(
        whiten_kernel,
        out_shape=jax.ShapeDtypeStruct((chans, GROUPS * depth), jnp.bfloat16),
        in_specs=[pl.BlockSpec(memory_space=pltpu.VMEM)] * 4,
        out_specs=pl.BlockSpec(memory_space=pltpu.VMEM),
        scratch_shapes=[
            pltpu.VMEM((PIECES, chans * windows, LANES), jnp.float32),
            pltpu.VMEM((GROUPS, 2, windows, GROUP, LANES), jnp.float32),
        ],
        compiler_params=pltpu.CompilerParams(vmem_limit_bytes=VMEM_LIMIT),
        cost_estimate=pl.CostEstimate(
            flops=2 * chans * windows * S * 2 * BINS, bytes_accessed=8_000_000, transcendentals=0
        ),
    )(traces, usable, jnp.asarray(dft_rows()), jnp.asarray(band_rows()))


def correlate_kernel(
    gram_steps, reach_ref, own_ref, near_ref, far_odd_ref, far_even_ref, lag_ref, out_ref, cross, slab
):
    chans = own_ref.shape[0]
    depth = own_ref.shape[1] // STEP_GROUPS
    half = depth // 2
    step = pl.program_id(0)

    @pl.when(step < gram_steps)
    def _():
        spot = lax.broadcasted_iota(jnp.int32, (GROUP, half), 1) % GROUP
        row = lax.broadcasted_iota(jnp.int32, (GROUP, half), 0)
        mask = (spot == row)[None]
        for g in range(STEP_GROUPS):
            columns = slice(g * depth, (g + 1) * depth)
            own = own_ref[:, columns]
            far = far_odd_ref[:, columns] + far_even_ref[:, columns]
            fill = jnp.zeros((SPAN - 3 * chans, depth), jnp.bfloat16)
            others = jnp.concatenate([own, near_ref[:, columns], far, fill], axis=0)
            value = own.astype(jnp.float32)
            real = jnp.where(mask, value[:, None, :half], 0.0)
            imag = jnp.where(mask, value[:, None, half:], 0.0)
            left = jnp.concatenate(
                [
                    jnp.concatenate([real, imag], axis=2),
                    jnp.concatenate([imag, -real], axis=2),
                ],
                axis=1,
            ).astype(jnp.bfloat16)
            products = lax.dot_general(
                left.reshape(chans * 2 * GROUP, depth),
                others,
                (((1,), (1,)), ((), ())),
                preferred_element_type=jnp.float32,
            )
            start = pl.multiple_of((step * STEP_GROUPS + g) * 2 * GROUP, 2 * GROUP)
            cross[:, pl.ds(start, 2 * GROUP), :] = products.astype(jnp.bfloat16).reshape(
                chans, 2 * GROUP, SPAN
            )

    @pl.when(step >= gram_steps)
    def _():
        offsets = lax.broadcasted_iota(jnp.int32, (R + 1, LAGS), 0)
        base = pl.multiple_of((step - gram_steps) * STEP_CHANS, STEP_CHANS)
        for j in range(STEP_CHANS):
            c = base + j
            lagged = jnp.dot(lag_ref[...], cross[c], preferred_element_type=jnp.float32)
            slab[j] = lagged.T
            band = slab.at[j, pl.ds(base, BAND), :][j : j + R + 1, :LAGS]
            out_ref[j] = jnp.where(offsets <= reach_ref[c], band, 0.0).astype(jnp.bfloat16)


def correlate(windows, reach, own, near, far_odd, far_even):
    chans, columns = own.shape
    gram_steps = GROUPS // STEP_GROUPS
    block = pl.BlockSpec(
        (chans, columns // gram_steps), lambda i: (0, jnp.minimum(i, gram_steps - 1))
    )

    def kernel(*refs):
        correlate_kernel(gram_steps, *refs)

    return pl.pallas_call(
        kernel,
        grid=(gram_steps + chans // STEP_CHANS,),
        out_shape=jax.ShapeDtypeStruct((chans, R + 1, LAGS), jnp.bfloat16),
        in_specs=[pl.BlockSpec(memory_space=pltpu.SMEM)]
        + [block] * 4
        + [pl.BlockSpec(memory_space=pltpu.VMEM)],
        out_specs=pl.BlockSpec(
            (STEP_CHANS, R + 1, LAGS), lambda i: (jnp.maximum(i - gram_steps, 0), 0, 0)
        ),
        scratch_shapes=[
            pltpu.VMEM((chans, 2 * F, SPAN), jnp.bfloat16),
            pltpu.VMEM((STEP_CHANS, SPAN, 256), jnp.float32),
        ],
        compiler_params=pltpu.CompilerParams(vmem_limit_bytes=VMEM_LIMIT),
        cost_estimate=pl.CostEstimate(
            flops=20_000_000_000, bytes_accessed=12_000_000, transcendentals=0
        ),
    )(reach, own, near, far_odd, far_even, jnp.asarray(lag_rows(windows)))


def local(traces, quality, reach):
    windows = traces.shape[1]
    count = lax.axis_size("chan")
    own = whiten(traces, quality)
    near = lax.ppermute(own, "chan", [(i, i - 1) for i in range(1, count)])
    far_odd = lax.ppermute(own, "chan", [(i, i - 2) for i in range(3, count, 2)])
    far_even = lax.ppermute(near, "chan", [(i, i - 1) for i in range(1, count, 2)])
    return correlate(windows, reach, own, near, far_odd, far_even)


def solution(mesh):
    return jax.shard_map(
        local,
        mesh=mesh,
        in_specs=(P(("day", "chan"), None, None), P(("day", "chan"), None), P(("day", "chan"))),
        out_specs=P(("day", "chan"), None, None),
        check_vma=False,
    )
```

time: 353 us -> 84.5 us (0.24)
  local copies, waits for them, and re-layouts: 107 us -> 8.76 us
  waiting for transfers between devices: 118 us -> 32.9 us
  matrix products: 81.2 us -> 0 us
  other arithmetic: 40 us -> 0.7 us
  Pallas kernels: 0 us -> 38.2 us
    ppermute x2 -> x3, waiting for transfers between devices: 118 us -> 32.9 us  [the longest x1 29.9 us: local(): lax.ppermute(near, 'chan', [(i, i - 1) for i in range(1, count, 2)])]
    dot_general x12 -> x0, matrix products: 81.2 us -> none  [the longest x8 41.5 us: batched_gram(): lax.dot_general(left_part, right_part, numbers, preferred_element_type=jn...]
    pallas_call x0 -> x2, Pallas kernels: none -> 38.2 us  [the longest x1 22 us: correlate(): pl.pallas_call(kernel, grid=(gram_steps + chans // STEP_CHANS,), out_shap...]
    another operation x4 -> x0, local copies, waits for them, and re-layouts: 34.7 us -> none
    concatenate x6 -> x0, local copies, waits for them, and re-layouts: 30.9 us -> none  [the longest x4 22.3 us: diagonals(): jnp.concatenate([flat, jnp.zeros((blocks, rows), jnp.float32)], axis=1)]
    reshape x4 -> x0, local copies, waits for them, and re-layouts: 27.7 us -> none  [diagonals(): return flat.reshape(blocks, rows, cols + 1)[:, :, :R + 1]]
    convert_element_type x2 -> x0, other arithmetic: 12.4 us -> none  [the longest x1 11.7 us: correlate(): jnp.where(keep[:, :, None], total / math.sqrt(F), 0.0).astype(jnp.bfloat16)]
    another operation x2 -> x0, other arithmetic: 10.9 us -> none
  transfers between devices with their start and end apart: 2 -> 3, of which waited for: 1 -> 2; matrix products, arithmetic and copies ran while one was open for 3% -> 0% of each run, Pallas kernels for 0% -> 0%
where the time goes in v1:
time: 84.5 us; the launch traced here: 84.1 us
  Pallas kernels  38.2 us (45%)
  waiting for transfers between devices  32.9 us (39%)
  local copies, waits for them, and re-layouts  8.76 us (10%)
  starting transfers between devices  3.49 us (4%)
    ppermute x1, waiting for transfers between devices, local(): lax.ppermute(near, 'chan', [(i, i - 1) for i in range(1, count, 2)])  29.9 us
    pallas_call x1, Pallas kernels, correlate(): pl.pallas_call(kernel, grid=(gram_steps + chans // STEP_CHANS,), out_shap...  22 us
    pallas_call x1, Pallas kernels, whiten(): pl.pallas_call(whiten_kernel, out_shape=jax.ShapeDtypeStruct((chans, GROU...  16.2 us
    pallas_call x1, local copies, waits for them, and re-layouts, correlate(): pl.pallas_call(kernel, grid=(gram_steps + chans // STEP_CHANS,), out_shap...  7.08 us
    ppermute x1, waiting for transfers between devices, local(): near = lax.ppermute(own, 'chan', [(i, i - 1) for i in range(1, count)])  3.09 us
  transfers between devices with their start and end apart: 3, of which 2 were waited for; matrix products, arithmetic and copies ran while one was open for 0% of the time, Pallas kernels for 0%

profile of v1, /device:TPU:0, one launch (start us, length us, event | category | flops | bytes accessed | tf_op | source)
XLA Modules:
  0.0 84.1 jit_solution(4406921545021673386)
XLA Ops:
  0.0 0.7 convert_bitcast_fusion
  0.7 0.6 pad.4
  1.3 16.2 %shard_map.64.refs_1_ = bf16[80,8192]{1,0:T(8,128)(2,1)} custom-call(bf16[80,16,1500]{2,1,0:T(8,128)(2,1)} %traces_ref.1, f32[1,2048]{1,0:T(1,128)} %bitcast.3, bf16[640,1536]{1,0:T(8,128)(2,1)} %constant.9.clone.dft_ref, bf16[256,320]{1,0:T(8,128)(2,1)} %constant.10.clone.band_ref), custom_call_target="tpu_custom_call" | custom-call | flops 2457600000 | bytes 8000000 | tf_op jit(solution)/shard_map/pallas_call | solution.py:107
  17.5 1.3 %collective-permute-start = (bf16[80,8192]{1,0:T(8,128)(2,1)}, bf16[80,8192]{1,0:T(8,128)(2,1)S(1)}, u32[]{:S(2)}, u32[]{:S(2)}) collective-permute-start(bf16[80,8192]{1,0:T(8,128)(2,1)} %shard_map.64.refs_1_), channel_id=1, source_target_pairs={{1,0},{2,1},{3,2},{4,3},{5,4},{6,5},{7,6},{8,7},{9,8},{10,9},{11,1... | collective-permute-start | bytes 3932168 | tf_op jit(solution)/shard_map/ppermute | solution.py:210
  18.8 0.7 collective-permute-start.1
  19.5 3.1 %collective-permute-done.refs_2_ = bf16[80,8192]{1,0:T(8,128)(2,1)S(1)} collective-permute-done((bf16[80,8192]{1,0:T(8,128)(2,1)}, bf16[80,8192]{1,0:T(8,128)(2,1)S(1)}, u32[]{:S(2)}, u32[]{:S(2)}) %collective-permute-start) | collective-permute-done | bytes 1310752 | tf_op jit(solution)/shard_map/ppermute | solution.py:210
  22.6 0.0 copy-start
  22.6 1.5 %collective-permute-start.2 = (bf16[80,8192]{1,0:T(8,128)(2,1)S(1)}, bf16[80,8192]{1,0:T(8,128)(2,1)S(1)}, u32[]{:S(2)}, u32[]{:S(2)}) collective-permute-start(bf16[80,8192]{1,0:T(8,128)(2,1)S(1)} %collective-permute-done.refs_2_), channel_id=1, source_target_pairs={{1,0},{3,2},{5,4},{7,6},{9,8},{11,10},{13,12},{15,14},{17,16},{19,... | collective-permute-start | bytes 3932168 | tf_op jit(solution)/shard_map/ppermute | solution.py:212
  24.1 0.0 collective-permute-done.1.refs_3_
  24.1 0.0 copy-start.1
  24.1 29.9 %collective-permute-done.2.refs_4_ = bf16[80,8192]{1,0:T(8,128)(2,1)S(1)} collective-permute-done((bf16[80,8192]{1,0:T(8,128)(2,1)S(1)}, bf16[80,8192]{1,0:T(8,128)(2,1)S(1)}, u32[]{:S(2)}, u32[]{:S(2)}) %collective-permute-start.2) | collective-permute-done | bytes 1310752 | tf_op jit(solution)/shard_map/ppermute | solution.py:212
  54.0 0.0 copy-done
  54.0 0.0 copy-done.1
  54.0 0.0 copy-start.2
  54.0 1.1 %copy-done.2 = bf16[80,8192]{1,0:T(8,128)(2,1)} copy-done((bf16[80,8192]{1,0:T(8,128)(2,1)}, bf16[80,8192]{1,0:T(8,128)(2,1)S(1)}, u32[]{:S(2)}) %copy-start.2) | copy-done | bytes 1310744
  55.0 22.0 %shard_map.65 = bf16[80,161,201]{2,1,0:T(8,128)(2,1)} custom-call(s32[80]{0:T(128)} %refs_0_.1, bf16[80,8192]{1,0:T(8,128)(2,1)} %shard_map.64.refs_1_, bf16[80,8192]{1,0:T(8,128)(2,1)} %copy-done, bf16[80,8192]{1,0:T(8,128)(2,1)} %copy-done.1, bf16[80,8192]{1,0:T(8,128)(2,1)} %copy-done.2, bf16[256,512]{1,0:T(8,128)(2,1)} %constant.11.clone.refs_5_), custom_call_target="tpu_custom_call" | custom-call | flops 20000000000 | bytes 12000000 | tf_op jit(solution)/shard_map/pallas_call | solution.py:185
  77.0 7.1 %copy.7 = bf16[80,161,201]{2,0,1:T(8,128)(2,1)} copy(bf16[80,161,201]{2,1,0:T(8,128)(2,1)} %shard_map.65) | data formatting | bytes 10355520 | tf_op jit(solution)/shard_map/pallas_call | solution.py:185
Async XLA Ops:
  17.5 5.1 %collective-permute-start = (bf16[80,8192]{1,0:T(8,128)(2,1)}, bf16[80,8192]{1,0:T(8,128)(2,1)S(1)}, u32[]{:S(2)}, u32[]{:S(2)}) collective-permute-start(bf16[80,8192]{1,0:T(8,128)(2,1)} %shard_map.64.refs_1_), channel_id=1, source_target_pairs={{1,0},{2,1},{3,2},{4,3},{5,4},{6,5},{7,6},{8,7},{9,8},{10,9},{11,1... | collective-permute-start | bytes 3932168 | tf_op jit(solution)/shard_map/ppermute | solution.py:210
  18.8 5.3 %collective-permute-start.1 = (bf16[80,8192]{1,0:T(8,128)(2,1)}, bf16[80,8192]{1,0:T(8,128)(2,1)S(1)}, u32[]{:S(2)}, u32[]{:S(2)}) collective-permute-start(bf16[80,8192]{1,0:T(8,128)(2,1)} %shard_map.64.refs_1_), channel_id=1, source_target_pairs={{3,1},{5,3},{7,5},{9,7},{11,9},{13,11},{15,13},{19,17},{21,19},{23... | collective-permute-start | bytes 3932168 | tf_op jit(solution)/shard_map/ppermute | solution.py:211
  22.6 31.4 %copy-start = (bf16[80,8192]{1,0:T(8,128)(2,1)}, bf16[80,8192]{1,0:T(8,128)(2,1)S(1)}, u32[]{:S(2)}) copy-start(bf16[80,8192]{1,0:T(8,128)(2,1)S(1)} %collective-permute-done.refs_2_) | copy-start | bytes 3932164
  22.6 31.4 %collective-permute-start.2 = (bf16[80,8192]{1,0:T(8,128)(2,1)S(1)}, bf16[80,8192]{1,0:T(8,128)(2,1)S(1)}, u32[]{:S(2)}, u32[]{:S(2)}) collective-permute-start(bf16[80,8192]{1,0:T(8,128)(2,1)S(1)} %collective-permute-done.refs_2_), channel_id=1, source_target_pairs={{1,0},{3,2},{5,4},{7,6},{9,8},{11,10},{13,12},{15,14},{17,16},{19,... | collective-permute-start | bytes 3932168 | tf_op jit(solution)/shard_map/ppermute | solution.py:212
  24.1 29.9 %copy-start.1 = (bf16[80,8192]{1,0:T(8,128)(2,1)}, bf16[80,8192]{1,0:T(8,128)(2,1)S(1)}, u32[]{:S(2)}) copy-start(bf16[80,8192]{1,0:T(8,128)(2,1)S(1)} %collective-permute-done.1.refs_3_) | copy-start | bytes 3932164
  54.0 1.1 %copy-start.2 = (bf16[80,8192]{1,0:T(8,128)(2,1)}, bf16[80,8192]{1,0:T(8,128)(2,1)S(1)}, u32[]{:S(2)}) copy-start(bf16[80,8192]{1,0:T(8,128)(2,1)S(1)} %collective-permute-done.2.refs_4_) | copy-start | bytes 3932164

commit v2 on v1

--- a/solution.py
+++ b/solution.py
@@ -19,10 +19,11 @@
 PIECES = -(-S // LANES)
 GROUP = 8
 GROUPS = F // GROUP
-BAND = 176
 SPAN = 256
 STEP_GROUPS = 4
-STEP_CHANS = 8
+STEP_CHANS = 16
+COLUMNS = 1024
+EARLY = 16
 VMEM_LIMIT = 56 * 1024 * 1024
 
 eps = 1e-06
@@ -55,7 +56,7 @@
     return np.concatenate([both, np.zeros((256 - LAGS, 2 * F), jnp.bfloat16)], axis=0)
 
 
-def whiten_kernel(traces_ref, quality_ref, dft_ref, band_ref, out_ref, wide, turned):
+def whiten_kernel(traces_ref, quality_ref, dft_ref, band_ref, first_ref, second_ref, wide, turned):
     chans, windows, _ = traces_ref.shape
     pieces = wide.shape[0]
     for c in range(0, chans, 8):
@@ -96,7 +97,11 @@
     depth = 2 * windows * GROUP
     for g in range(GROUPS):
         block = turned[g].reshape(depth, LANES).T
-        out_ref[:, g * depth : (g + 1) * depth] = block[:chans].astype(jnp.bfloat16)
+        block = block[:chans].astype(jnp.bfloat16)
+        if g < EARLY:
+            first_ref[:, g * depth : (g + 1) * depth] = block
+        else:
+            second_ref[:, (g - EARLY) * depth : (g - EARLY + 1) * depth] = block
 
 
 def whiten(traces, quality):
@@ -106,9 +111,12 @@
     depth = 2 * windows * GROUP
     return pl.pallas_call(
         whiten_kernel,
-        out_shape=jax.ShapeDtypeStruct((chans, GROUPS * depth), jnp.bfloat16),
+        out_shape=[
+            jax.ShapeDtypeStruct((chans, EARLY * depth), jnp.bfloat16),
+            jax.ShapeDtypeStruct((chans, (GROUPS - EARLY) * depth), jnp.bfloat16),
+        ],
         in_specs=[pl.BlockSpec(memory_space=pltpu.VMEM)] * 4,
-        out_specs=pl.BlockSpec(memory_space=pltpu.VMEM),
+        out_specs=[pl.BlockSpec(memory_space=pltpu.VMEM)] * 2,
         scratch_shapes=[
             pltpu.VMEM((PIECES, chans * windows, LANES), jnp.float32),
             pltpu.VMEM((GROUPS, 2, windows, GROUP, LANES), jnp.float32),
@@ -120,97 +128,188 @@
     )(traces, usable, jnp.asarray(dft_rows()), jnp.asarray(band_rows()))
 
 
-def correlate_kernel(
-    gram_steps, reach_ref, own_ref, near_ref, far_odd_ref, far_even_ref, lag_ref, out_ref, cross, slab
-):
+def gram(own_ref, near_ref, far_odd_ref, far_even_ref, store):
     chans = own_ref.shape[0]
     depth = own_ref.shape[1] // STEP_GROUPS
     half = depth // 2
+    spot = lax.broadcasted_iota(jnp.int32, (GROUP, half), 1) % GROUP
+    row = lax.broadcasted_iota(jnp.int32, (GROUP, half), 0)
+    mask = (spot == row)[None]
+    for g in range(STEP_GROUPS):
+        columns = slice(g * depth, (g + 1) * depth)
+        own = own_ref[:, columns]
+        far = far_odd_ref[:, columns] + far_even_ref[:, columns]
+        fill = jnp.zeros((SPAN - 3 * chans, depth), jnp.bfloat16)
+        others = jnp.concatenate([own, near_ref[:, columns], far, fill], axis=0)
+        value = own.astype(jnp.float32)
+        real = jnp.where(mask, value[:, None, :half], 0.0)
+        imag = jnp.where(mask, value[:, None, half:], 0.0)
+        left = jnp.concatenate(
+            [
+                jnp.concatenate([real, imag], axis=2),
+                jnp.concatenate([imag, -real], axis=2),
+            ],
+            axis=1,
+        ).astype(jnp.bfloat16)
+        products = lax.dot_general(
+            left.reshape(chans * 2 * GROUP, depth),
+            others,
+            (((1,), (1,)), ((), ())),
+            preferred_element_type=jnp.float32,
+        )
+        store(g, products.astype(jnp.bfloat16).reshape(chans, 2 * GROUP, SPAN))
+
+
+def early_kernel(own_ref, near_ref, far_odd_ref, far_even_ref, cross_ref):
+    def store(g, products):
+        cross_ref[:, g * 2 * GROUP : (g + 1) * 2 * GROUP, :] = products
+
+    gram(own_ref, near_ref, far_odd_ref, far_even_ref, store)
+
+
+def early_cross(own, near, far_odd, far_even):
+    chans, columns = own.shape
+    steps = columns // COLUMNS
+    block = pl.BlockSpec((chans, COLUMNS), lambda i: (0, i))
+    rows = STEP_GROUPS * 2 * GROUP
+    return pl.pallas_call(
+        early_kernel,
+        grid=(steps,),
+        out_shape=jax.ShapeDtypeStruct((chans, steps * rows, SPAN), jnp.bfloat16),
+        in_specs=[block] * 4,
+        out_specs=pl.BlockSpec((chans, rows, SPAN), lambda i: (0, i, 0)),
+        compiler_params=pltpu.CompilerParams(vmem_limit_bytes=VMEM_LIMIT),
+        cost_estimate=pl.CostEstimate(
+            flops=8_000_000_000, bytes_accessed=13_000_000, transcendentals=0
+        ),
+    )(own, near, far_odd, far_even)
+
+
+def late_kernel(
+    gram_steps,
+    reach_ref,
+    own_ref,
+    near_ref,
+    far_odd_ref,
+    far_even_ref,
+    early_ref,
+    lag_ref,
+    out_ref,
+    cross,
+    turned,
+):
+    chans = own_ref.shape[0]
     step = pl.program_id(0)
 
     @pl.when(step < gram_steps)
     def _():
-        spot = lax.broadcasted_iota(jnp.int32, (GROUP, half), 1) % GROUP
-        row = lax.broadcasted_iota(jnp.int32, (GROUP, half), 0)
-        mask = (spot == row)[None]
-        for g in range(STEP_GROUPS):
-            columns = slice(g * depth, (g + 1) * depth)
-            own = own_ref[:, columns]
-            far = far_odd_ref[:, columns] + far_even_ref[:, columns]
-            fill = jnp.zeros((SPAN - 3 * chans, depth), jnp.bfloat16)
-            others = jnp.concatenate([own, near_ref[:, columns], far, fill], axis=0)
-            value = own.astype(jnp.float32)
-            real = jnp.where(mask, value[:, None, :half], 0.0)
-            imag = jnp.where(mask, value[:, None, half:], 0.0)
-            left = jnp.concatenate(
-                [
-                    jnp.concatenate([real, imag], axis=2),
-                    jnp.concatenate([imag, -real], axis=2),
-                ],
-                axis=1,
-            ).astype(jnp.bfloat16)
-            products = lax.dot_general(
-                left.reshape(chans * 2 * GROUP, depth),
-                others,
-                (((1,), (1,)), ((), ())),
-                preferred_element_type=jnp.float32,
-            )
+        def store(g, products):
             start = pl.multiple_of((step * STEP_GROUPS + g) * 2 * GROUP, 2 * GROUP)
-            cross[:, pl.ds(start, 2 * GROUP), :] = products.astype(jnp.bfloat16).reshape(
-                chans, 2 * GROUP, SPAN
-            )
+            cross[:, pl.ds(start, 2 * GROUP), :] = products
+
+        gram(own_ref, near_ref, far_odd_ref, far_even_ref, store)
 
     @pl.when(step >= gram_steps)
     def _():
-        offsets = lax.broadcasted_iota(jnp.int32, (R + 1, LAGS), 0)
-        base = pl.multiple_of((step - gram_steps) * STEP_CHANS, STEP_CHANS)
+        depth = early_ref.shape[1]
+        base = (step - gram_steps) * STEP_CHANS
         for j in range(STEP_CHANS):
             c = base + j
-            lagged = jnp.dot(lag_ref[...], cross[c], preferred_element_type=jnp.float32)
-            slab[j] = lagged.T
-            band = slab.at[j, pl.ds(base, BAND), :][j : j + R + 1, :LAGS]
-            out_ref[j] = jnp.where(offsets <= reach_ref[c], band, 0.0).astype(jnp.bfloat16)
-
-
-def correlate(windows, reach, own, near, far_odd, far_even):
+            lagged = jnp.dot(lag_ref[:, :depth], early_ref[j], preferred_element_type=jnp.float32)
+            lagged = lagged + jnp.dot(
+                lag_ref[:, depth:], cross[c], preferred_element_type=jnp.float32
+            )
+            start = (chans - c) * STEP_CHANS + j
+            for p in range(2):
+                part = lagged[p * LANES : (p + 1) * LANES].T
+                turned[p, pl.ds(start, SPAN, stride=STEP_CHANS), :] = part
+        first = chans * STEP_CHANS
+        last = first + (R + 1) * STEP_CHANS
+        offsets = lax.broadcasted_iota(jnp.int32, (R + 1, STEP_CHANS, LANES), 0)
+        keep = offsets <= reach_ref[...][None]
+        for p in range(2):
+            width = min(LANES, LAGS - p * LANES)
+            part = turned[p, first:last, :].reshape(R + 1, STEP_CHANS, LANES)
+            part = jnp.where(keep, part, 0.0).astype(jnp.bfloat16)
+            out_ref[:, :, p * LANES : p * LANES + width] = part[:, :, :width]
+
+
+def late_correlate(windows, reach, own, near, far_odd, far_even, early):
     chans, columns = own.shape
-    gram_steps = GROUPS // STEP_GROUPS
-    block = pl.BlockSpec(
-        (chans, columns // gram_steps), lambda i: (0, jnp.minimum(i, gram_steps - 1))
-    )
+    gram_steps = columns // COLUMNS
+    depth = early.shape[1]
+    block = pl.BlockSpec((chans, COLUMNS), lambda i: (0, jnp.minimum(i, gram_steps - 1)))
+
+    def later(i):
+        return jnp.maximum(i - gram_steps, 0)
 
     def kernel(*refs):
-        correlate_kernel(gram_steps, *refs)
-
-    return pl.pallas_call(
+        late_kernel(gram_steps, *refs)
+
+    turned = pl.pallas_call(
         kernel,
         grid=(gram_steps + chans // STEP_CHANS,),
-        out_shape=jax.ShapeDtypeStruct((chans, R + 1, LAGS), jnp.bfloat16),
-        in_specs=[pl.BlockSpec(memory_space=pltpu.SMEM)]
+        out_shape=jax.ShapeDtypeStruct((R + 1, chans, LAGS), jnp.bfloat16),
+        in_specs=[pl.BlockSpec((STEP_CHANS, LANES), lambda i: (later(i), 0))]
         + [block] * 4
+        + [pl.BlockSpec((STEP_CHANS, depth, SPAN), lambda i: (later(i), 0, 0))]
         + [pl.BlockSpec(memory_space=pltpu.VMEM)],
-        out_specs=pl.BlockSpec(
-            (STEP_CHANS, R + 1, LAGS), lambda i: (jnp.maximum(i - gram_steps, 0), 0, 0)
-        ),
+        out_specs=pl.BlockSpec((R + 1, STEP_CHANS, LAGS), lambda i: (0, later(i), 0)),
         scratch_shapes=[
-            pltpu.VMEM((chans, 2 * F, SPAN), jnp.bfloat16),
-            pltpu.VMEM((STEP_CHANS, SPAN, 256), jnp.float32),
+            pltpu.VMEM((chans, 2 * F - depth, SPAN), jnp.bfloat16),
+            pltpu.VMEM((2, (chans + SPAN) * STEP_CHANS, LANES), jnp.float32),
         ],
         compiler_params=pltpu.CompilerParams(vmem_limit_bytes=VMEM_LIMIT),
         cost_estimate=pl.CostEstimate(
-            flops=20_000_000_000, bytes_accessed=12_000_000, transcendentals=0
+            flops=12_000_000_000, bytes_accessed=20_000_000, transcendentals=0
         ),
-    )(reach, own, near, far_odd, far_even, jnp.asarray(lag_rows(windows)))
+    )(
+        jnp.broadcast_to(reach[:, None], (chans, LANES)),
+        own,
+        near,
+        far_odd,
+        far_even,
+        early,
+        jnp.asarray(lag_rows(windows)),
+    )
+    return jnp.transpose(turned, (1, 0, 2))
+
+
+def follow_kernel(value_ref, near_ref, far_ref, out_ref):
+    pass
+
+
+def follow(value, near, far):
+    return pl.pallas_call(
+        follow_kernel,
+        out_shape=jax.ShapeDtypeStruct(value.shape, value.dtype),
+        in_specs=[pl.BlockSpec(memory_space=pl.ANY)] * 3,
+        out_specs=pl.BlockSpec(memory_space=pl.ANY),
+        input_output_aliases={0: 0},
+    )(value, near, far)
+
+
+def neighbours(own):
+    count = lax.axis_size("chan")
+    near = lax.ppermute(own, "chan", [(i, i - 1) for i in range(1, count)])
+    far_odd = lax.ppermute(own, "chan", [(i, i - 2) for i in range(3, count, 2)])
+    return near, far_odd
+
+
+def relayed(near):
+    count = lax.axis_size("chan")
+    return lax.ppermute(near, "chan", [(i, i - 1) for i in range(1, count, 2)])
 
 
 def local(traces, quality, reach):
     windows = traces.shape[1]
-    count = lax.axis_size("chan")
-    own = whiten(traces, quality)
-    near = lax.ppermute(own, "chan", [(i, i - 1) for i in range(1, count)])
-    far_odd = lax.ppermute(own, "chan", [(i, i - 2) for i in range(3, count, 2)])
-    far_even = lax.ppermute(near, "chan", [(i, i - 1) for i in range(1, count, 2)])
-    return correlate(windows, reach, own, near, far_odd, far_even)
+    first, second = whiten(traces, quality)
+    near, far_odd = neighbours(first)
+    second = follow(second, near, far_odd)
+    early = early_cross(first, near, far_odd, relayed(near))
+    near, far_odd = neighbours(second)
+    near = follow(near, early, early)
+    return late_correlate(windows, reach, second, near, far_odd, relayed(near), early)
 
 
 def solution(mesh):

time: 84.5 us -> 87.4 us (1.034)
  Pallas kernels: 38.2 us -> 48.2 us
  waiting for transfers between devices: 32.9 us -> 27.3 us
  local copies, waits for them, and re-layouts: 8.76 us -> 3.98 us
  starting transfers between devices: 3.49 us -> 6.71 us
    pallas_call x2 -> x5, Pallas kernels: 38.2 us -> 48.2 us  [the longest x1 24.4 us: late_correlate(): pl.pallas_call(kernel, grid=(gram_steps + chans // STEP_CHANS,), out_shap...]
    pallas_call x1 -> x0, local copies, waits for them, and re-layouts: 7.08 us -> none  [correlate(): pl.pallas_call(kernel, grid=(gram_steps + chans // STEP_CHANS,), out_shap...]
    ppermute x3 -> x6, waiting for transfers between devices: 32.9 us -> 27.3 us  [the longest x2 25.1 us: relayed(): return lax.ppermute(near, 'chan', [(i, i - 1) for i in range(1, count, 2)])]
    ppermute x3 -> x6, starting transfers between devices: 3.49 us -> 6.71 us  [the longest x2 2.74 us: relayed(): return lax.ppermute(near, 'chan', [(i, i - 1) for i in range(1, count, 2)])]
    unnamed x6 -> x14, local copies, waits for them, and re-layouts: 1.08 us -> 2.59 us
  transfers between devices with their start and end apart: 3 -> 6, of which waited for: 2 -> 3; matrix products, arithmetic and copies ran while one was open for 0% -> 0% of each run, Pallas kernels for 0% -> 9%
where the time goes in v2:
time: 87.4 us; the launch traced here: 86.9 us
  Pallas kernels  48.2 us (55%)
  waiting for transfers between devices  27.3 us (31%)
  starting transfers between devices  6.71 us (8%)
  local copies, waits for them, and re-layouts  3.98 us (5%)
    ppermute x2, waiting for transfers between devices, relayed(): return lax.ppermute(near, 'chan', [(i, i - 1) for i in range(1, count, 2)])  25.1 us
    pallas_call x1, Pallas kernels, late_correlate(): pl.pallas_call(kernel, grid=(gram_steps + chans // STEP_CHANS,), out_shap...  24.4 us
    pallas_call x1, Pallas kernels, whiten(): pl.pallas_call(whiten_kernel, out_shape=[jax.ShapeDtypeStruct((chans, EAR...  16 us
    pallas_call x1, Pallas kernels, early_cross(): pl.pallas_call(early_kernel, grid=(steps,), out_shape=jax.ShapeDtypeStruc...  7.74 us
    ppermute x2, starting transfers between devices, relayed(): return lax.ppermute(near, 'chan', [(i, i - 1) for i in range(1, count, 2)])  2.74 us
    unnamed x14, local copies, waits for them, and re-layouts  2.59 us
    ppermute x2, starting transfers between devices, neighbours(): near = lax.ppermute(own, 'chan', [(i, i - 1) for i in range(1, count)])  2.57 us
    ppermute x2, waiting for transfers between devices, neighbours(): near = lax.ppermute(own, 'chan', [(i, i - 1) for i in range(1, count)])  2.19 us
  transfers between devices with their start and end apart: 6, of which 3 were waited for; matrix products, arithmetic and copies ran while one was open for 0% of the time, Pallas kernels for 9%

profile of v2, /device:TPU:0, one launch (start us, length us, event | category | flops | bytes accessed | tf_op | source)
XLA Modules:
  0.0 86.9 jit_solution(14066301049428256187)
XLA Ops:
  0.0 0.7 convert_bitcast_fusion
  0.7 0.6 pad.4
  1.3 16.0 %shard_map.64 = (bf16[80,4096]{1,0:T(8,128)(2,1)}, bf16[80,4096]{1,0:T(8,128)(2,1)}) custom-call(bf16[80,16,1500]{2,1,0:T(8,128)(2,1)} %traces_ref.1, f32[1,2048]{1,0:T(1,128)} %bitcast.4, bf16[640,1536]{1,0:T(8,128)(2,1)} %constant.9.clone.dft_ref, bf16[256,320]{1,0:T(8,128)(2,1)} %constant.10.clone.band_ref), custom_call_target="tpu_custom_call" | custom-call | flops 2457600000 | bytes 8000000 | tf_op jit(solution)/shard_map/pallas_call | solution.py:112
  17.3 1.3 %collective-permute-start = (bf16[80,4096]{1,0:T(8,128)(2,1)}, bf16[80,4096]{1,0:T(8,128)(2,1)S(1)}, u32[]{:S(2)}, u32[]{:S(2)}) collective-permute-start(bf16[80,4096]{1,0:T(8,128)(2,1)} %get-tuple-element.8.own_ref), channel_id=1, source_target_pairs={{1,0},{2,1},{3,2},{4,3},{5,4},{6,5},{7,6},{8,7},{9,8},{10,9},{11,1... | collective-permute-start | bytes 1966088 | tf_op jit(solution)/shard_map/ppermute | solution.py:294
  18.6 0.7 collective-permute-start.1
  19.3 2.2 %collective-permute-done.near_ref = bf16[80,4096]{1,0:T(8,128)(2,1)S(1)} collective-permute-done((bf16[80,4096]{1,0:T(8,128)(2,1)}, bf16[80,4096]{1,0:T(8,128)(2,1)S(1)}, u32[]{:S(2)}, u32[]{:S(2)}) %collective-permute-start) | collective-permute-done | bytes 655392 | tf_op jit(solution)/shard_map/ppermute | solution.py:294
  21.5 0.0 copy-start.1
  21.5 1.3 %collective-permute-start.3 = (bf16[80,4096]{1,0:T(8,128)(2,1)S(1)}, bf16[80,4096]{1,0:T(8,128)(2,1)S(1)}, u32[]{:S(2)}, u32[]{:S(2)}) collective-permute-start(bf16[80,4096]{1,0:T(8,128)(2,1)S(1)} %collective-permute-done.near_ref), channel_id=1, source_target_pairs={{1,0},{3,2},{5,4},{7,6},{9,8},{11,10},{13,12},{15,14},{17,16},{19,... | collective-permute-start | bytes 1966088 | tf_op jit(solution)/shard_map/ppermute | solution.py:301
  22.8 0.0 collective-permute-done.1.far_ref.far_odd_ref
  22.8 0.0 copy-start.2
  22.8 0.0 copy-done.1
  22.8 0.8 copy-done.2
  23.6 0.7 collective-permute-start.4
  24.3 1.3 %collective-permute-start.2 = (bf16[80,4096]{1,0:T(8,128)(2,1)}, bf16[80,4096]{1,0:T(8,128)(2,1)S(1)}, u32[]{:S(2)}, u32[]{:S(2)}) collective-permute-start(bf16[80,4096]{1,0:T(8,128)(2,1)} %shard_map.65.refs_1_), channel_id=1, source_target_pairs={{1,0},{2,1},{3,2},{4,3},{5,4},{6,5},{7,6},{8,7},{9,8},{10,9},{11,1... | collective-permute-start | bytes 1966088 | tf_op jit(solution)/shard_map/ppermute | solution.py:294
  25.6 13.2 %collective-permute-done.3.far_even_ref = bf16[80,4096]{1,0:T(8,128)(2,1)S(1)} collective-permute-done((bf16[80,4096]{1,0:T(8,128)(2,1)S(1)}, bf16[80,4096]{1,0:T(8,128)(2,1)S(1)}, u32[]{:S(2)}, u32[]{:S(2)}) %collective-permute-start.3) | collective-permute-done | bytes 655392 | tf_op jit(solution)/shard_map/ppermute | solution.py:301
  38.8 0.0 copy-start.5
  38.8 0.9 copy-done.5
  39.6 7.7 %shard_map.66.near_ref.far_ref.refs_5_ = bf16[80,256,256]{2,1,0:T(8,128)(2,1)} custom-call(bf16[80,4096]{1,0:T(8,128)(2,1)} %get-tuple-element.8.own_ref, bf16[80,4096]{1,0:T(8,128)(2,1)} %copy-done.1, bf16[80,4096]{1,0:T(8,128)(2,1)} %copy-done.2, bf16[80,4096]{1,0:T(8,128)(2,1)} %copy-done.5), custom_call_target="tpu_custom_call" | custom-call | flops 8000000000 | bytes 13000000 | tf_op jit(solution)/shard_map/pallas_call | solution.py:175
  47.4 0.0 copy-start.3
  47.4 0.0 collective-permute-done.2.value_ref
  47.4 0.0 copy-start
  47.4 0.9 copy-done
  48.3 1.5 %collective-permute-start.5 = (bf16[80,4096]{1,0:T(8,128)(2,1)}, bf16[80,4096]{1,0:T(8,128)(2,1)S(1)}, u32[]{:S(2)}, u32[]{:S(2)}) collective-permute-start(bf16[80,4096]{1,0:T(8,128)(2,1)} %shard_map.67.refs_2_), channel_id=1, source_target_pairs={{1,0},{3,2},{5,4},{7,6},{9,8},{11,10},{13,12},{15,14},{17,16},{19,... | collective-permute-start | bytes 1966088 | tf_op jit(solution)/shard_map/ppermute | solution.py:301
  49.7 0.0 collective-permute-done.4.refs_3_
  49.7 0.0 copy-start.4
  49.7 11.9 %collective-permute-done.5.refs_4_ = bf16[80,4096]{1,0:T(8,128)(2,1)S(1)} collective-permute-done((bf16[80,4096]{1,0:T(8,128)(2,1)}, bf16[80,4096]{1,0:T(8,128)(2,1)S(1)}, u32[]{:S(2)}, u32[]{:S(2)}) %collective-permute-start.5) | collective-permute-done | bytes 655392 | tf_op jit(solution)/shard_map/ppermute | solution.py:301
  61.7 0.0 copy-done.3
  61.7 0.0 copy-start.6
  61.7 0.8 broadcast_in_dim.2.refs_0_
  62.4 0.0 copy-done.4
  62.4 0.1 copy-done.6
  62.5 24.4 %shard_map.68 = bf16[161,80,201]{2,1,0:T(8,128)(2,1)} custom-call(s32[80,128]{1,0:T(8,128)} %broadcast_in_dim.2.refs_0_, bf16[80,4096]{1,0:T(8,128)(2,1)} %shard_map.65.refs_1_, bf16[80,4096]{1,0:T(8,128)(2,1)} %shard_map.67.refs_2_, bf16[80,4096]{1,0:T(8,128)(2,1)} %copy-done.4, bf16[80,4096]{1,0:T(8,128)(2,1)} %copy-done.6, ...), custom_call_target="tpu_custom_call" | custom-call | flops 12000000000 | bytes 20000000 | tf_op jit(solution)/shard_map/pallas_call | solution.py:249
  (2 shorter events, 0.0 us)
Async XLA Ops:
  17.3 4.2 %collective-permute-start = (bf16[80,4096]{1,0:T(8,128)(2,1)}, bf16[80,4096]{1,0:T(8,128)(2,1)S(1)}, u32[]{:S(2)}, u32[]{:S(2)}) collective-permute-start(bf16[80,4096]{1,0:T(8,128)(2,1)} %get-tuple-element.8.own_ref), channel_id=1, source_target_pairs={{1,0},{2,1},{3,2},{4,3},{5,4},{6,5},{7,6},{8,7},{9,8},{10,9},{11,1... | collective-permute-start | bytes 1966088 | tf_op jit(solution)/shard_map/ppermute | solution.py:294
  18.6 4.2 %collective-permute-start.1 = (bf16[80,4096]{1,0:T(8,128)(2,1)}, bf16[80,4096]{1,0:T(8,128)(2,1)S(1)}, u32[]{:S(2)}, u32[]{:S(2)}) collective-permute-start(bf16[80,4096]{1,0:T(8,128)(2,1)} %get-tuple-element.8.own_ref), channel_id=1, source_target_pairs={{3,1},{5,3},{7,5},{9,7},{11,9},{13,11},{15,13},{19,17},{21,19},{23... | collective-permute-start | bytes 1966088 | tf_op jit(solution)/shard_map/ppermute | solution.py:295
  21.5 1.3 %copy-start.1 = (bf16[80,4096]{1,0:T(8,128)(2,1)}, bf16[80,4096]{1,0:T(8,128)(2,1)S(1)}, u32[]{:S(2)}) copy-start(bf16[80,4096]{1,0:T(8,128)(2,1)S(1)} %collective-permute-done.near_ref) | copy-start | bytes 1966084
  21.5 17.3 %collective-permute-start.3 = (bf16[80,4096]{1,0:T(8,128)(2,1)S(1)}, bf16[80,4096]{1,0:T(8,128)(2,1)S(1)}, u32[]{:S(2)}, u32[]{:S(2)}) collective-permute-start(bf16[80,4096]{1,0:T(8,128)(2,1)S(1)} %collective-permute-done.near_ref), channel_id=1, source_target_pairs={{1,0},{3,2},{5,4},{7,6},{9,8},{11,10},{13,12},{15,14},{17,16},{19,... | collective-permute-start | bytes 1966088 | tf_op jit(solution)/shard_map/ppermute | solution.py:301
  22.8 0.8 copy-start.2
  23.6 26.1 %collective-permute-start.4 = (bf16[80,4096]{1,0:T(8,128)(2,1)}, bf16[80,4096]{1,0:T(8,128)(2,1)S(1)}, u32[]{:S(2)}, u32[]{:S(2)}) collective-permute-start(bf16[80,4096]{1,0:T(8,128)(2,1)} %shard_map.65.refs_1_), channel_id=1, source_target_pairs={{3,1},{5,3},{7,5},{9,7},{11,9},{13,11},{15,13},{19,17},{21,19},{23... | collective-permute-start | bytes 1966088 | tf_op jit(solution)/shard_map/ppermute | solution.py:295
  24.3 23.1 %collective-permute-start.2 = (bf16[80,4096]{1,0:T(8,128)(2,1)}, bf16[80,4096]{1,0:T(8,128)(2,1)S(1)}, u32[]{:S(2)}, u32[]{:S(2)}) collective-permute-start(bf16[80,4096]{1,0:T(8,128)(2,1)} %shard_map.65.refs_1_), channel_id=1, source_target_pairs={{1,0},{2,1},{3,2},{4,3},{5,4},{6,5},{7,6},{8,7},{9,8},{10,9},{11,1... | collective-permute-start | bytes 1966088 | tf_op jit(solution)/shard_map/ppermute | solution.py:294
  38.8 0.9 copy-start.5
  47.4 14.3 %copy-start.3 = (s32[80]{0:T(128)S(1)}, s32[80]{0:T(128)}, u32[]{:S(2)}) copy-start(s32[80]{0:T(128)} %param.8) | copy-start | bytes 964
  47.4 0.9 copy-start
  48.3 13.4 %collective-permute-start.5 = (bf16[80,4096]{1,0:T(8,128)(2,1)}, bf16[80,4096]{1,0:T(8,128)(2,1)S(1)}, u32[]{:S(2)}, u32[]{:S(2)}) collective-permute-start(bf16[80,4096]{1,0:T(8,128)(2,1)} %shard_map.67.refs_2_), channel_id=1, source_target_pairs={{1,0},{3,2},{5,4},{7,6},{9,8},{11,10},{13,12},{15,14},{17,16},{19,... | collective-permute-start | bytes 1966088 | tf_op jit(solution)/shard_map/ppermute | solution.py:301
  49.7 12.7 %copy-start.4 = (bf16[80,4096]{1,0:T(8,128)(2,1)}, bf16[80,4096]{1,0:T(8,128)(2,1)S(1)}, u32[]{:S(2)}) copy-start(bf16[80,4096]{1,0:T(8,128)(2,1)S(1)} %collective-permute-done.4.refs_3_) | copy-start | bytes 1966084
  61.7 0.8 copy-start.6

commit v3 on v2

--- a/solution.py
+++ b/solution.py
@@ -22,6 +22,7 @@
 SPAN = 256
 STEP_GROUPS = 4
 STEP_CHANS = 16
+PITCH = STEP_CHANS + 1
 COLUMNS = 1024
 EARLY = 16
 VMEM_LIMIT = 56 * 1024 * 1024
@@ -29,18 +30,18 @@
 eps = 1e-06
 
 
-def dft_rows():
+def dft_rows(first, last):
     times = np.arange(S, dtype=np.int32)
-    bins = 1 + np.arange(BINS, dtype=np.int32)
+    bins = 1 + np.arange(first, last + 2 * HALF_SMOOTH, dtype=np.int32)
     phase = bins[:, None] * times[None, :] % S
     angle = np.float32(2.0 * math.pi / S) * phase.astype(np.float32)
     table = np.concatenate([np.cos(angle), -np.sin(angle)], axis=0)
     return np.pad(table, ((0, 0), (0, PIECES * LANES - S))).astype(jnp.bfloat16)
 
 
-def band_rows():
-    outer = np.arange(F)[:, None]
-    inner = np.arange(BINS)[None, :]
+def band_rows(count):
+    outer = np.arange(count)[:, None]
+    inner = np.arange(count + 2 * HALF_SMOOTH)[None, :]
     return ((inner >= outer) & (inner <= outer + 2 * HALF_SMOOTH)).astype(jnp.bfloat16)
 
 
@@ -56,30 +57,35 @@
     return np.concatenate([both, np.zeros((256 - LAGS, 2 * F), jnp.bfloat16)], axis=0)
 
 
-def whiten_kernel(traces_ref, quality_ref, dft_ref, band_ref, first_ref, second_ref, wide, turned):
+def arrange(traces_ref, rows_ref, wide):
     chans, windows, _ = traces_ref.shape
     pieces = wide.shape[0]
-    for c in range(0, chans, 8):
-        rows = traces_ref[c : c + 8].astype(jnp.float32).reshape(8 * windows, S)
+    pitch = windows + 1
+    for c in range(chans):
+        rows = traces_ref[c].astype(jnp.float32)
         for p in range(pieces):
             piece = rows[:, p * LANES : (p + 1) * LANES]
             if piece.shape[1] < LANES:
-                rest = jnp.zeros((8 * windows, LANES - piece.shape[1]), jnp.float32)
+                rest = jnp.zeros((windows, LANES - piece.shape[1]), jnp.float32)
                 piece = jnp.concatenate([piece, rest], axis=1)
-            wide[p, c * windows : (c + 8) * windows, :] = piece
-    fill = jnp.zeros((LANES - chans, pieces * LANES), jnp.bfloat16)
-
-    def window(w):
-        rows = [wide[p, pl.ds(w, chans, stride=windows), :] for p in range(pieces)]
-        return jnp.concatenate(rows, axis=1).astype(jnp.bfloat16)
-
+            wide[p, c * pitch : c * pitch + windows, :] = piece
+    for w in range(windows):
+        for p in range(pieces):
+            piece = wide[p, pl.ds(w, chans, stride=pitch), :]
+            rows_ref[w, :, p * LANES : (p + 1) * LANES] = piece.astype(jnp.bfloat16)
+
+
+def whiten_rows(rows_ref, quality_ref, dft_ref, band_ref, out_ref, turned):
+    windows, chans, samples = rows_ref.shape
+    count, bins = band_ref.shape
+    fill = jnp.zeros((LANES - chans, samples), jnp.bfloat16)
     for w in range(0, windows, 2):
-        both = jnp.concatenate([window(w), fill, window(w + 1), fill], axis=0)
+        both = jnp.concatenate([rows_ref[w], fill, rows_ref[w + 1], fill], axis=0)
         spectra = lax.dot_general(
             dft_ref[...], both, (((1,), (1,)), ((), ())), preferred_element_type=jnp.float32
         )
-        real = spectra[:BINS]
-        imag = spectra[BINS:]
+        real = spectra[:bins]
+        imag = spectra[bins:]
         amplitude = jnp.sqrt(real * real + imag * imag)
         high = amplitude.astype(jnp.bfloat16)
         low = (amplitude - high.astype(jnp.float32)).astype(jnp.bfloat16)
@@ -88,44 +94,46 @@
         scale = 1.0 / (smooth * (1.0 / (2 * HALF_SMOOTH + 1)) + eps)
         usable = quality_ref[:, w * LANES : (w + 2) * LANES]
         scale = scale * usable
-        real = real[HALF_SMOOTH : HALF_SMOOTH + F] * scale
-        imag = imag[HALF_SMOOTH : HALF_SMOOTH + F] * scale
+        real = real[HALF_SMOOTH : HALF_SMOOTH + count] * scale
+        imag = imag[HALF_SMOOTH : HALF_SMOOTH + count] * scale
         for j in range(2):
             lanes = slice(j * LANES, (j + 1) * LANES)
-            turned[:, 0, w + j] = real[:, lanes].reshape(GROUPS, GROUP, LANES)
-            turned[:, 1, w + j] = imag[:, lanes].reshape(GROUPS, GROUP, LANES)
+            turned[:, 0, w + j] = real[:, lanes].reshape(count // GROUP, GROUP, LANES)
+            turned[:, 1, w + j] = imag[:, lanes].reshape(count // GROUP, GROUP, LANES)
     depth = 2 * windows * GROUP
-    for g in range(GROUPS):
+    for g in range(count // GROUP):
         block = turned[g].reshape(depth, LANES).T
-        block = block[:chans].astype(jnp.bfloat16)
-        if g < EARLY:
-            first_ref[:, g * depth : (g + 1) * depth] = block
-        else:
-            second_ref[:, (g - EARLY) * depth : (g - EARLY + 1) * depth] = block
-
-
-def whiten(traces, quality):
-    chans, windows, _ = traces.shape
-    usable = jnp.pad(quality.astype(jnp.float32).T, ((0, 0), (0, LANES - chans)))
-    usable = usable.reshape(1, windows * LANES)
+        out_ref[:, g * depth : (g + 1) * depth] = block[:chans].astype(jnp.bfloat16)
+
+
+def first_kernel(traces_ref, quality_ref, dft_ref, band_ref, out_ref, rows_ref, turned, wide):
+    arrange(traces_ref, rows_ref, wide)
+    whiten_rows(rows_ref, quality_ref, dft_ref, band_ref, out_ref, turned)
+
+
+def whiten(source, usable, first, last, arranged):
+    windows = usable.shape[1] // LANES
+    chans = source.shape[1] if arranged else source.shape[0]
+    groups = (last - first) // GROUP
+    bins = last - first + 2 * HALF_SMOOTH
     depth = 2 * windows * GROUP
+    whole = pl.BlockSpec(memory_space=pltpu.VMEM)
+    out = [jax.ShapeDtypeStruct((chans, groups * depth), jnp.bfloat16)]
+    scratch = [pltpu.VMEM((groups, 2, windows, GROUP, LANES), jnp.float32)]
+    if not arranged:
+        out.append(jax.ShapeDtypeStruct((windows, chans, PIECES * LANES), jnp.bfloat16))
+        scratch.append(pltpu.VMEM((PIECES, chans * (windows + 1), LANES), jnp.float32))
     return pl.pallas_call(
-        whiten_kernel,
-        out_shape=[
-            jax.ShapeDtypeStruct((chans, EARLY * depth), jnp.bfloat16),
-            jax.ShapeDtypeStruct((chans, (GROUPS - EARLY) * depth), jnp.bfloat16),
-        ],
-        in_specs=[pl.BlockSpec(memory_space=pltpu.VMEM)] * 4,
-        out_specs=[pl.BlockSpec(memory_space=pltpu.VMEM)] * 2,
-        scratch_shapes=[
-            pltpu.VMEM((PIECES, chans * windows, LANES), jnp.float32),
-            pltpu.VMEM((GROUPS, 2, windows, GROUP, LANES), jnp.float32),
-        ],
+        whiten_rows if arranged else first_kernel,
+        out_shape=out,
+        in_specs=[whole] * 4,
+        out_specs=[whole] * len(out),
+        scratch_shapes=scratch,
         compiler_params=pltpu.CompilerParams(vmem_limit_bytes=VMEM_LIMIT),
         cost_estimate=pl.CostEstimate(
-            flops=2 * chans * windows * S * 2 * BINS, bytes_accessed=8_000_000, transcendentals=0
+            flops=4 * chans * windows * S * bins, bytes_accessed=8_000_000, transcendentals=0
         ),
-    )(traces, usable, jnp.asarray(dft_rows()), jnp.asarray(band_rows()))
+    )(source, usable, jnp.asarray(dft_rows(first, last)), jnp.asarray(band_rows(last - first)))
 
 
 def gram(own_ref, near_ref, far_odd_ref, far_even_ref, store):
@@ -219,19 +227,17 @@
             lagged = lagged + jnp.dot(
                 lag_ref[:, depth:], cross[c], preferred_element_type=jnp.float32
             )
-            start = (chans - c) * STEP_CHANS + j
+            start = (chans - c) * PITCH + j
             for p in range(2):
                 part = lagged[p * LANES : (p + 1) * LANES].T
-                turned[p, pl.ds(start, SPAN, stride=STEP_CHANS), :] = part
-        first = chans * STEP_CHANS
-        last = first + (R + 1) * STEP_CHANS
-        offsets = lax.broadcasted_iota(jnp.int32, (R + 1, STEP_CHANS, LANES), 0)
-        keep = offsets <= reach_ref[...][None]
-        for p in range(2):
-            width = min(LANES, LAGS - p * LANES)
-            part = turned[p, first:last, :].reshape(R + 1, STEP_CHANS, LANES)
-            part = jnp.where(keep, part, 0.0).astype(jnp.bfloat16)
-            out_ref[:, :, p * LANES : p * LANES + width] = part[:, :, :width]
+                turned[p, pl.ds(start, SPAN, stride=PITCH), :] = part
+        reach = reach_ref[...]
+        for k in range(R + 1):
+            start = (chans + k) * PITCH
+            for p in range(2):
+                width = min(LANES, LAGS - p * LANES)
+                part = jnp.where(reach >= k, turned[p, start : start + STEP_CHANS, :], 0.0)
+                out_ref[k, :, p * LANES : p * LANES + width] = part[:, :width].astype(jnp.bfloat16)
 
 
 def late_correlate(windows, reach, own, near, far_odd, far_even, early):
@@ -257,7 +263,7 @@
         out_specs=pl.BlockSpec((R + 1, STEP_CHANS, LAGS), lambda i: (0, later(i), 0)),
         scratch_shapes=[
             pltpu.VMEM((chans, 2 * F - depth, SPAN), jnp.bfloat16),
-            pltpu.VMEM((2, (chans + SPAN) * STEP_CHANS, LANES), jnp.float32),
+            pltpu.VMEM((2, (chans + SPAN) * PITCH, LANES), jnp.float32),
         ],
         compiler_params=pltpu.CompilerParams(vmem_limit_bytes=VMEM_LIMIT),
         cost_estimate=pl.CostEstimate(
@@ -303,13 +309,18 @@
 
 def local(traces, quality, reach):
     windows = traces.shape[1]
-    first, second = whiten(traces, quality)
+    chans = traces.shape[0]
+    usable = jnp.pad(quality.astype(jnp.float32).T, ((0, 0), (0, LANES - chans)))
+    usable = usable.reshape(1, windows * LANES)
+    split = EARLY * GROUP
+    first, rows = whiten(traces, usable, 0, split, False)
     near, far_odd = neighbours(first)
-    second = follow(second, near, far_odd)
+    (second,) = whiten(rows, usable, split, F, True)
+    next_near, next_odd = neighbours(second)
+    near = follow(near, second, second)
     early = early_cross(first, near, far_odd, relayed(near))
-    near, far_odd = neighbours(second)
-    near = follow(near, early, early)
-    return late_correlate(windows, reach, second, near, far_odd, relayed(near), early)
+    near = follow(next_near, early, early)
+    return late_correlate(windows, reach, second, near, next_odd, relayed(near), early)
 
 
 def solution(mesh):

time: 87.4 us -> 74.4 us (0.85)
  waiting for transfers between devices: 27.3 us -> 16.2 us
  Pallas kernels: 48.2 us -> 46.1 us
    ppermute x2, waiting for transfers between devices: 25.1 us -> 16.2 us  [relayed(): return lax.ppermute(near, 'chan', [(i, i - 1) for i in range(1, count, 2)])]
    pallas_call x1, Pallas kernels: 24.4 us -> 16.8 us  [late_correlate(): pl.pallas_call(kernel, grid=(gram_steps + chans // STEP_CHANS,), out_shap...]
    pallas_call x1 -> x2, Pallas kernels: 16 us -> 21.5 us  [whiten(): pl.pallas_call(whiten_rows if arranged else first_kernel, out_shape=out,...]
    ppermute x2, waiting for transfers between devices: 2.19 us -> 0.01 us  [neighbours(): near = lax.ppermute(own, 'chan', [(i, i - 1) for i in range(1, count)])]
  transfers between devices with their start and end apart: 6 -> 6, of which waited for: 3 -> 2; matrix products, arithmetic and copies ran while one was open for 0% -> 0% of each run, Pallas kernels for 9% -> 24%
where the time goes in v3:
time: 74.4 us; the launch traced here: 73.9 us
  Pallas kernels  46.1 us (62%)
  waiting for transfers between devices  16.2 us (22%)
  starting transfers between devices  6.72 us (9%)
  local copies, waits for them, and re-layouts  4.04 us (5%)
    pallas_call x2, Pallas kernels, whiten(): pl.pallas_call(whiten_rows if arranged else first_kernel, out_shape=out,...  21.5 us
    pallas_call x1, Pallas kernels, late_correlate(): pl.pallas_call(kernel, grid=(gram_steps + chans // STEP_CHANS,), out_shap...  16.8 us
    ppermute x2, waiting for transfers between devices, relayed(): return lax.ppermute(near, 'chan', [(i, i - 1) for i in range(1, count, 2)])  16.2 us
    pallas_call x1, Pallas kernels, early_cross(): pl.pallas_call(early_kernel, grid=(steps,), out_shape=jax.ShapeDtypeStruc...  7.74 us
    ppermute x2, starting transfers between devices, relayed(): return lax.ppermute(near, 'chan', [(i, i - 1) for i in range(1, count, 2)])  2.74 us
    unnamed x14, local copies, waits for them, and re-layouts  2.65 us
    ppermute x2, starting transfers between devices, neighbours(): near = lax.ppermute(own, 'chan', [(i, i - 1) for i in range(1, count)])  2.57 us
  transfers between devices with their start and end apart: 6, of which 2 were waited for; matrix products, arithmetic and copies ran while one was open for 0% of the time, Pallas kernels for 24%

profile of v3, /device:TPU:0, one launch (start us, length us, event | category | flops | bytes accessed | tf_op | source)
XLA Modules:
  0.0 73.9 jit_solution(1100360405041449241)
XLA Ops:
  0.0 0.7 convert_bitcast_fusion
  0.7 0.6 pad.4
  1.3 11.2 %shard_map.82 = (bf16[80,4096]{1,0:T(8,128)(2,1)}, bf16[16,80,1536]{2,1,0:T(8,128)(2,1)}) custom-call(bf16[80,16,1500]{2,1,0:T(8,128)(2,1)} %traces_ref.1, f32[1,2048]{1,0:T(1,128)} %bitcast.4, bf16[384,1536]{1,0:T(8,128)(2,1)} %constant.11.clone.dft_ref, bf16[128,192]{1,0:T(8,128)(2,1)} %constant.12.clone.band_ref), custom_call_target="tpu_custom_call" | custom-call | flops 1474560000 | bytes 8000000 | tf_op jit(solution)/shard_map/pallas_call | solution.py:126
  12.5 1.3 %collective-permute-start.1 = (bf16[80,4096]{1,0:T(8,128)(2,1)}, bf16[80,4096]{1,0:T(8,128)(2,1)S(1)}, u32[]{:S(2)}, u32[]{:S(2)}) collective-permute-start(bf16[80,4096]{1,0:T(8,128)(2,1)} %get-tuple-element.8.own_ref), channel_id=1, source_target_pairs={{1,0},{2,1},{3,2},{4,3},{5,4},{6,5},{7,6},{8,7},{9,8},{10,9},{11,1... | collective-permute-start | bytes 1966088 | tf_op jit(solution)/shard_map/ppermute | solution.py:300
  13.8 0.7 collective-permute-start.2
  14.5 10.3 %shard_map.83.near_ref.far_ref.refs_1_ = bf16[80,4096]{1,0:T(8,128)(2,1)} custom-call(bf16[16,80,1536]{2,1,0:T(8,128)(2,1)} %get-tuple-element.7.rows_ref, f32[1,2048]{1,0:T(1,128)} %bitcast.5, bf16[384,1536]{1,0:T(8,128)(2,1)} %constant.13.clone.dft_ref, bf16[128,192]{1,0:T(8,128)(2,1)} %constant.12.clone.band_ref), custom_call_target="tpu_custom_call" | custom-call | flops 1474560000 | bytes 8000000 | tf_op jit(solution)/shard_map/pallas_call | solution.py:126
  24.8 0.0 collective-permute-done.1.value_ref
  24.8 0.0 copy-start.1
  24.8 0.8 %copy-done.1 = bf16[80,4096]{1,0:T(8,128)(2,1)} copy-done((bf16[80,4096]{1,0:T(8,128)(2,1)}, bf16[80,4096]{1,0:T(8,128)(2,1)S(1)}, u32[]{:S(2)}) %copy-start.1) | copy-done | bytes 655384
  25.6 1.3 %collective-permute-start.3 = (bf16[80,4096]{1,0:T(8,128)(2,1)}, bf16[80,4096]{1,0:T(8,128)(2,1)S(1)}, u32[]{:S(2)}, u32[]{:S(2)}) collective-permute-start(bf16[80,4096]{1,0:T(8,128)(2,1)} %shard_map.84.near_ref), channel_id=1, source_target_pairs={{1,0},{3,2},{5,4},{7,6},{9,8},{11,10},{13,12},{15,14},{17,16},{19,... | collective-permute-start | bytes 1966088 | tf_op jit(solution)/shard_map/ppermute | solution.py:307
  26.9 0.7 collective-permute-start.4
  27.6 1.3 %collective-permute-start = (bf16[80,4096]{1,0:T(8,128)(2,1)}, bf16[80,4096]{1,0:T(8,128)(2,1)S(1)}, u32[]{:S(2)}, u32[]{:S(2)}) collective-permute-start(bf16[80,4096]{1,0:T(8,128)(2,1)} %shard_map.83.near_ref.far_ref.refs_1_), channel_id=1, source_target_pairs={{1,0},{2,1},{3,2},{4,3},{5,4},{6,5},{7,6},{8,7},{9,8},{10,9},{11,1... | collective-permute-start | bytes 1966088 | tf_op jit(solution)/shard_map/ppermute | solution.py:300
  28.9 0.0 collective-permute-done.2.far_odd_ref
  29.0 0.0 copy-start.4
  29.0 6.1 %collective-permute-done.3.far_even_ref = bf16[80,4096]{1,0:T(8,128)(2,1)S(1)} collective-permute-done((bf16[80,4096]{1,0:T(8,128)(2,1)}, bf16[80,4096]{1,0:T(8,128)(2,1)S(1)}, u32[]{:S(2)}, u32[]{:S(2)}) %collective-permute-start.3) | collective-permute-done | bytes 655392 | tf_op jit(solution)/shard_map/ppermute | solution.py:307
  35.1 0.0 copy-done.4
  35.1 0.0 copy-start.5
  35.1 0.9 %copy-done.5 = bf16[80,4096]{1,0:T(8,128)(2,1)} copy-done((bf16[80,4096]{1,0:T(8,128)(2,1)}, bf16[80,4096]{1,0:T(8,128)(2,1)S(1)}, u32[]{:S(2)}) %copy-start.5) | copy-done | bytes 655384
  35.9 7.7 %shard_map.85.near_ref.far_ref.refs_5_ = bf16[80,256,256]{2,1,0:T(8,128)(2,1)} custom-call(bf16[80,4096]{1,0:T(8,128)(2,1)} %get-tuple-element.8.own_ref, bf16[80,4096]{1,0:T(8,128)(2,1)} %shard_map.84.near_ref, bf16[80,4096]{1,0:T(8,128)(2,1)} %copy-done.4, bf16[80,4096]{1,0:T(8,128)(2,1)} %copy-done.5), custom_call_target="tpu_custom_call" | custom-call | flops 8000000000 | bytes 13000000 | tf_op jit(solution)/shard_map/pallas_call | solution.py:183
  43.7 0.0 copy-start.2
  43.7 0.0 collective-permute-done.value_ref
  43.7 0.0 copy-start
  43.7 0.9 %copy-done = bf16[80,4096]{1,0:T(8,128)(2,1)} copy-done((bf16[80,4096]{1,0:T(8,128)(2,1)}, bf16[80,4096]{1,0:T(8,128)(2,1)S(1)}, u32[]{:S(2)}) %copy-start) | copy-done | bytes 655384
  44.5 1.5 %collective-permute-start.5 = (bf16[80,4096]{1,0:T(8,128)(2,1)}, bf16[80,4096]{1,0:T(8,128)(2,1)S(1)}, u32[]{:S(2)}, u32[]{:S(2)}) collective-permute-start(bf16[80,4096]{1,0:T(8,128)(2,1)} %shard_map.86.refs_2_), channel_id=1, source_target_pairs={{1,0},{3,2},{5,4},{7,6},{9,8},{11,10},{13,12},{15,14},{17,16},{19,... | collective-permute-start | bytes 1966088 | tf_op jit(solution)/shard_map/ppermute | solution.py:307
  46.0 0.0 collective-permute-done.4.refs_3_
  46.0 0.0 copy-start.3
  46.0 10.1 %collective-permute-done.5.refs_4_ = bf16[80,4096]{1,0:T(8,128)(2,1)S(1)} collective-permute-done((bf16[80,4096]{1,0:T(8,128)(2,1)}, bf16[80,4096]{1,0:T(8,128)(2,1)S(1)}, u32[]{:S(2)}, u32[]{:S(2)}) %collective-permute-start.5) | collective-permute-done | bytes 655392 | tf_op jit(solution)/shard_map/ppermute | solution.py:307
  56.1 0.0 copy-done.2
  56.2 0.0 copy-start.6
  56.2 0.8 %broadcast_in_dim.2.refs_0_ = s32[80,128]{1,0:T(8,128)} broadcast(s32[80]{0:T(128)S(1)} %copy-done.2), dimensions={0} | broadcast | bytes 41280 | tf_op jit(solution)/shard_map/broadcast_in_dim | solution.py:273
  56.9 0.0 copy-done.3
  56.9 0.1 copy-done.6
  57.0 16.8 %shard_map.87 = bf16[161,80,201]{2,1,0:T(8,128)(2,1)} custom-call(s32[80,128]{1,0:T(8,128)} %broadcast_in_dim.2.refs_0_, bf16[80,4096]{1,0:T(8,128)(2,1)} %shard_map.83.near_ref.far_ref.refs_1_, bf16[80,4096]{1,0:T(8,128)(2,1)} %shard_map.86.refs_2_, bf16[80,4096]{1,0:T(8,128)(2,1)} %copy-done.3, bf16[80,4096]{1,0:T(8,128)(2,1)} %copy-done.6, ...), custom_call_target="tpu_custom_call" | custom-call | flops 12000000000 | bytes 20000000 | tf_op jit(solution)/shard_map/pallas_call | solution.py:255
  (2 shorter events, 0.0 us)
Async XLA Ops:
  12.5 12.3 %collective-permute-start.1 = (bf16[80,4096]{1,0:T(8,128)(2,1)}, bf16[80,4096]{1,0:T(8,128)(2,1)S(1)}, u32[]{:S(2)}, u32[]{:S(2)}) collective-permute-start(bf16[80,4096]{1,0:T(8,128)(2,1)} %get-tuple-element.8.own_ref), channel_id=1, source_target_pairs={{1,0},{2,1},{3,2},{4,3},{5,4},{6,5},{7,6},{8,7},{9,8},{10,9},{11,1... | collective-permute-start | bytes 1966088 | tf_op jit(solution)/shard_map/ppermute | solution.py:300
  13.8 15.1 %collective-permute-start.2 = (bf16[80,4096]{1,0:T(8,128)(2,1)}, bf16[80,4096]{1,0:T(8,128)(2,1)S(1)}, u32[]{:S(2)}, u32[]{:S(2)}) collective-permute-start(bf16[80,4096]{1,0:T(8,128)(2,1)} %get-tuple-element.8.own_ref), channel_id=1, source_target_pairs={{3,1},{5,3},{7,5},{9,7},{11,9},{13,11},{15,13},{19,17},{21,19},{23... | collective-permute-start | bytes 1966088 | tf_op jit(solution)/shard_map/ppermute | solution.py:301
  24.8 0.8 %copy-start.1 = (bf16[80,4096]{1,0:T(8,128)(2,1)}, bf16[80,4096]{1,0:T(8,128)(2,1)S(1)}, u32[]{:S(2)}) copy-start(bf16[80,4096]{1,0:T(8,128)(2,1)S(1)} %collective-permute-done.1.value_ref) | copy-start | bytes 1966084
  25.6 9.4 %collective-permute-start.3 = (bf16[80,4096]{1,0:T(8,128)(2,1)}, bf16[80,4096]{1,0:T(8,128)(2,1)S(1)}, u32[]{:S(2)}, u32[]{:S(2)}) collective-permute-start(bf16[80,4096]{1,0:T(8,128)(2,1)} %shard_map.84.near_ref), channel_id=1, source_target_pairs={{1,0},{3,2},{5,4},{7,6},{9,8},{11,10},{13,12},{15,14},{17,16},{19,... | collective-permute-start | bytes 1966088 | tf_op jit(solution)/shard_map/ppermute | solution.py:307
  26.9 19.1 %collective-permute-start.4 = (bf16[80,4096]{1,0:T(8,128)(2,1)}, bf16[80,4096]{1,0:T(8,128)(2,1)S(1)}, u32[]{:S(2)}, u32[]{:S(2)}) collective-permute-start(bf16[80,4096]{1,0:T(8,128)(2,1)} %shard_map.83.near_ref.far_ref.refs_1_), channel_id=1, source_target_pairs={{3,1},{5,3},{7,5},{9,7},{11,9},{13,11},{15,13},{19,17},{21,19},{23... | collective-permute-start | bytes 1966088 | tf_op jit(solution)/shard_map/ppermute | solution.py:301
  27.6 16.0 %collective-permute-start = (bf16[80,4096]{1,0:T(8,128)(2,1)}, bf16[80,4096]{1,0:T(8,128)(2,1)S(1)}, u32[]{:S(2)}, u32[]{:S(2)}) collective-permute-start(bf16[80,4096]{1,0:T(8,128)(2,1)} %shard_map.83.near_ref.far_ref.refs_1_), channel_id=1, source_target_pairs={{1,0},{2,1},{3,2},{4,3},{5,4},{6,5},{7,6},{8,7},{9,8},{10,9},{11,1... | collective-permute-start | bytes 1966088 | tf_op jit(solution)/shard_map/ppermute | solution.py:300
  29.0 6.1 %copy-start.4 = (bf16[80,4096]{1,0:T(8,128)(2,1)}, bf16[80,4096]{1,0:T(8,128)(2,1)S(1)}, u32[]{:S(2)}) copy-start(bf16[80,4096]{1,0:T(8,128)(2,1)S(1)} %collective-permute-done.2.far_odd_ref) | copy-start | bytes 1966084
  35.1 0.9 %copy-start.5 = (bf16[80,4096]{1,0:T(8,128)(2,1)}, bf16[80,4096]{1,0:T(8,128)(2,1)S(1)}, u32[]{:S(2)}) copy-start(bf16[80,4096]{1,0:T(8,128)(2,1)S(1)} %collective-permute-done.3.far_even_ref) | copy-start | bytes 1966084
  43.7 12.5 %copy-start.2 = (s32[80]{0:T(128)S(1)}, s32[80]{0:T(128)}, u32[]{:S(2)}) copy-start(s32[80]{0:T(128)} %param.10) | copy-start | bytes 964
  43.7 0.9 %copy-start = (bf16[80,4096]{1,0:T(8,128)(2,1)}, bf16[80,4096]{1,0:T(8,128)(2,1)S(1)}, u32[]{:S(2)}) copy-start(bf16[80,4096]{1,0:T(8,128)(2,1)S(1)} %collective-permute-done.value_ref) | copy-start | bytes 1966084
  44.5 11.6 %collective-permute-start.5 = (bf16[80,4096]{1,0:T(8,128)(2,1)}, bf16[80,4096]{1,0:T(8,128)(2,1)S(1)}, u32[]{:S(2)}, u32[]{:S(2)}) collective-permute-start(bf16[80,4096]{1,0:T(8,128)(2,1)} %shard_map.86.refs_2_), channel_id=1, source_target_pairs={{1,0},{3,2},{5,4},{7,6},{9,8},{11,10},{13,12},{15,14},{17,16},{19,... | collective-permute-start | bytes 1966088 | tf_op jit(solution)/shard_map/ppermute | solution.py:307
  46.0 10.9 %copy-start.3 = (bf16[80,4096]{1,0:T(8,128)(2,1)}, bf16[80,4096]{1,0:T(8,128)(2,1)S(1)}, u32[]{:S(2)}) copy-start(bf16[80,4096]{1,0:T(8,128)(2,1)S(1)} %collective-permute-done.4.refs_3_) | copy-start | bytes 1966084
  56.2 0.9 %copy-start.6 = (bf16[80,4096]{1,0:T(8,128)(2,1)}, bf16[80,4096]{1,0:T(8,128)(2,1)S(1)}, u32[]{:S(2)}) copy-start(bf16[80,4096]{1,0:T(8,128)(2,1)S(1)} %collective-permute-done.5.refs_4_) | copy-start | bytes 1966084

commit v4 on v3

--- a/solution.py
+++ b/solution.py
@@ -12,7 +12,6 @@
 S = 1500
 F = 256
 HALF_SMOOTH = 32
-BINS = F + 2 * HALF_SMOOTH
 LAG = 100
 LAGS = 2 * LAG + 1
 LANES = 128
@@ -24,25 +23,32 @@
 STEP_CHANS = 16
 PITCH = STEP_CHANS + 1
 COLUMNS = 1024
-EARLY = 16
+WHITEN_CHANS = 16
 VMEM_LIMIT = 56 * 1024 * 1024
 
 eps = 1e-06
 
 
-def dft_rows(first, last):
+def dft_columns(first):
     times = np.arange(S, dtype=np.int32)
-    bins = 1 + np.arange(first, last + 2 * HALF_SMOOTH, dtype=np.int32)
-    phase = bins[:, None] * times[None, :] % S
-    angle = np.float32(2.0 * math.pi / S) * phase.astype(np.float32)
-    table = np.concatenate([np.cos(angle), -np.sin(angle)], axis=0)
-    return np.pad(table, ((0, 0), (0, PIECES * LANES - S))).astype(jnp.bfloat16)
-
-
-def band_rows(count):
-    outer = np.arange(count)[:, None]
-    inner = np.arange(count + 2 * HALF_SMOOTH)[None, :]
-    return ((inner >= outer) & (inner <= outer + 2 * HALF_SMOOTH)).astype(jnp.bfloat16)
+    own = first + HALF_SMOOTH + np.arange(LANES)
+    sides = first + np.concatenate([np.arange(HALF_SMOOTH), LANES + HALF_SMOOTH + np.arange(HALF_SMOOTH)])
+
+    def columns(bins):
+        phase = times[:, None] * (1 + bins[None, :]).astype(np.int32) % S
+        angle = np.float32(2.0 * math.pi / S) * phase.astype(np.float32)
+        rest = ((0, PIECES * LANES - S), (0, LANES - bins.size))
+        return [np.pad(part, rest) for part in (np.cos(angle), -np.sin(angle))]
+
+    return np.concatenate(columns(own) + columns(sides), axis=1).astype(jnp.bfloat16)
+
+
+def band_columns():
+    rows = np.arange(LANES + 2 * HALF_SMOOTH)
+    order = np.concatenate([rows[HALF_SMOOTH:-HALF_SMOOTH], rows[:HALF_SMOOTH], rows[-HALF_SMOOTH:]])
+    outer = np.arange(LANES)[None, :]
+    inside = (order[:, None] >= outer) & (order[:, None] <= outer + 2 * HALF_SMOOTH)
+    return np.pad(inside, ((0, LANES - 2 * HALF_SMOOTH), (0, 0))).astype(jnp.bfloat16)
 
 
 def lag_rows(windows):
@@ -57,83 +63,65 @@
     return np.concatenate([both, np.zeros((256 - LAGS, 2 * F), jnp.bfloat16)], axis=0)
 
 
-def arrange(traces_ref, rows_ref, wide):
-    chans, windows, _ = traces_ref.shape
-    pieces = wide.shape[0]
+def whiten_kernel(traces_ref, quality_ref, dft_ref, band_ref, out_ref, wide):
+    chans, windows, samples = traces_ref.shape
     pitch = windows + 1
-    for c in range(chans):
-        rows = traces_ref[c].astype(jnp.float32)
-        for p in range(pieces):
-            piece = rows[:, p * LANES : (p + 1) * LANES]
-            if piece.shape[1] < LANES:
-                rest = jnp.zeros((windows, LANES - piece.shape[1]), jnp.float32)
-                piece = jnp.concatenate([piece, rest], axis=1)
-            wide[p, c * pitch : c * pitch + windows, :] = piece
-    for w in range(windows):
-        for p in range(pieces):
-            piece = wide[p, pl.ds(w, chans, stride=pitch), :]
-            rows_ref[w, :, p * LANES : (p + 1) * LANES] = piece.astype(jnp.bfloat16)
-
-
-def whiten_rows(rows_ref, quality_ref, dft_ref, band_ref, out_ref, turned):
-    windows, chans, samples = rows_ref.shape
-    count, bins = band_ref.shape
-    fill = jnp.zeros((LANES - chans, samples), jnp.bfloat16)
-    for w in range(0, windows, 2):
-        both = jnp.concatenate([rows_ref[w], fill, rows_ref[w + 1], fill], axis=0)
-        spectra = lax.dot_general(
-            dft_ref[...], both, (((1,), (1,)), ((), ())), preferred_element_type=jnp.float32
-        )
-        real = spectra[:bins]
-        imag = spectra[bins:]
-        amplitude = jnp.sqrt(real * real + imag * imag)
-        high = amplitude.astype(jnp.bfloat16)
-        low = (amplitude - high.astype(jnp.float32)).astype(jnp.bfloat16)
-        smooth = jnp.dot(band_ref[...], high, preferred_element_type=jnp.float32)
-        smooth = smooth + jnp.dot(band_ref[...], low, preferred_element_type=jnp.float32)
-        scale = 1.0 / (smooth * (1.0 / (2 * HALF_SMOOTH + 1)) + eps)
-        usable = quality_ref[:, w * LANES : (w + 2) * LANES]
-        scale = scale * usable
-        real = real[HALF_SMOOTH : HALF_SMOOTH + count] * scale
-        imag = imag[HALF_SMOOTH : HALF_SMOOTH + count] * scale
-        for j in range(2):
-            lanes = slice(j * LANES, (j + 1) * LANES)
-            turned[:, 0, w + j] = real[:, lanes].reshape(count // GROUP, GROUP, LANES)
-            turned[:, 1, w + j] = imag[:, lanes].reshape(count // GROUP, GROUP, LANES)
-    depth = 2 * windows * GROUP
-    for g in range(count // GROUP):
-        block = turned[g].reshape(depth, LANES).T
-        out_ref[:, g * depth : (g + 1) * depth] = block[:chans].astype(jnp.bfloat16)
-
-
-def first_kernel(traces_ref, quality_ref, dft_ref, band_ref, out_ref, rows_ref, turned, wide):
-    arrange(traces_ref, rows_ref, wide)
-    whiten_rows(rows_ref, quality_ref, dft_ref, band_ref, out_ref, turned)
-
-
-def whiten(source, usable, first, last, arranged):
-    windows = usable.shape[1] // LANES
-    chans = source.shape[1] if arranged else source.shape[0]
-    groups = (last - first) // GROUP
-    bins = last - first + 2 * HALF_SMOOTH
-    depth = 2 * windows * GROUP
+    rows = traces_ref[...].reshape(chans * windows, samples)
+    rest = jnp.zeros((chans * windows, PIECES * LANES - samples), jnp.bfloat16)
+    rows = jnp.concatenate([rows, rest], axis=1)
+    spectra = jnp.dot(rows, dft_ref[...], preferred_element_type=jnp.float32)
+    own = [spectra[:, :LANES], spectra[:, LANES : 2 * LANES]]
+    sides = [spectra[:, 2 * LANES : 3 * LANES], spectra[:, 3 * LANES :]]
+    amplitude = jnp.concatenate(
+        [jnp.sqrt(real * real + imag * imag) for real, imag in (own, sides)], axis=1
+    )
+    high = amplitude.astype(jnp.bfloat16)
+    low = (amplitude - high.astype(jnp.float32)).astype(jnp.bfloat16)
+    smooth = jnp.dot(high, band_ref[...], preferred_element_type=jnp.float32)
+    smooth = smooth + jnp.dot(low, band_ref[...], preferred_element_type=jnp.float32)
+    scale = quality_ref[...] / (smooth * (1.0 / (2 * HALF_SMOOTH + 1)) + eps)
+    place = lax.broadcasted_iota(jnp.int32, (chans, LANES), 1) // GROUP
+    for i in range(2):
+        value = own[i] * scale
+        for c in range(chans):
+            wide[i, c * pitch : c * pitch + windows, :] = value[c * windows : (c + 1) * windows]
+        turned = []
+        for n in range(windows):
+            w = (windows - n) % windows
+            turned.append(pltpu.roll(wide[i, pl.ds(w, chans, stride=pitch), :], w * GROUP, 1))
+        shift = 1
+        while shift < windows:
+            moves = (place // shift) % 2 == 1
+            turned = [
+                jnp.where(moves, turned[(n - shift) % windows], turned[n]) for n in range(windows)
+            ]
+            shift *= 2
+        for g in range(windows):
+            start = (2 * g + i) * LANES
+            out_ref[:, start : start + LANES] = turned[g].astype(jnp.bfloat16)
+
+
+def whiten(traces, usable, first):
+    chans, windows, _ = traces.shape
+    columns = 2 * LANES * windows
     whole = pl.BlockSpec(memory_space=pltpu.VMEM)
-    out = [jax.ShapeDtypeStruct((chans, groups * depth), jnp.bfloat16)]
-    scratch = [pltpu.VMEM((groups, 2, windows, GROUP, LANES), jnp.float32)]
-    if not arranged:
-        out.append(jax.ShapeDtypeStruct((windows, chans, PIECES * LANES), jnp.bfloat16))
-        scratch.append(pltpu.VMEM((PIECES, chans * (windows + 1), LANES), jnp.float32))
     return pl.pallas_call(
-        whiten_rows if arranged else first_kernel,
-        out_shape=out,
-        in_specs=[whole] * 4,
-        out_specs=[whole] * len(out),
-        scratch_shapes=scratch,
+        whiten_kernel,
+        grid=(chans // WHITEN_CHANS,),
+        out_shape=jax.ShapeDtypeStruct((chans, columns), jnp.bfloat16),
+        in_specs=[
+            pl.BlockSpec((WHITEN_CHANS, windows, S), lambda i: (i, 0, 0)),
+            pl.BlockSpec((WHITEN_CHANS * windows, LANES), lambda i: (i, 0)),
+            whole,
+            whole,
+        ],
+        out_specs=pl.BlockSpec((WHITEN_CHANS, columns), lambda i: (i, 0)),
+        scratch_shapes=[pltpu.VMEM((2, WHITEN_CHANS * (windows + 1), LANES), jnp.float32)],
         compiler_params=pltpu.CompilerParams(vmem_limit_bytes=VMEM_LIMIT),
         cost_estimate=pl.CostEstimate(
-            flops=4 * chans * windows * S * bins, bytes_accessed=8_000_000, transcendentals=0
+            flops=8 * chans * windows * S * LANES, bytes_accessed=8_000_000, transcendentals=0
         ),
-    )(source, usable, jnp.asarray(dft_rows(first, last)), jnp.asarray(band_rows(last - first)))
+    )(traces, usable, jnp.asarray(dft_columns(first)), jnp.asarray(band_columns()))
 
 
 def gram(own_ref, near_ref, far_odd_ref, far_even_ref, store):
@@ -309,13 +297,11 @@
 
 def local(traces, quality, reach):
     windows = traces.shape[1]
-    chans = traces.shape[0]
-    usable = jnp.pad(quality.astype(jnp.float32).T, ((0, 0), (0, LANES - chans)))
-    usable = usable.reshape(1, windows * LANES)
-    split = EARLY * GROUP
-    first, rows = whiten(traces, usable, 0, split, False)
+    usable = quality.astype(jnp.float32).reshape(-1, 1)
+    usable = jnp.broadcast_to(usable, (usable.shape[0], LANES))
+    first = whiten(traces, usable, 0)
     near, far_odd = neighbours(first)
-    (second,) = whiten(rows, usable, split, F, True)
+    second = whiten(traces, usable, LANES)
     next_near, next_odd = neighbours(second)
     near = follow(near, second, second)
     early = early_cross(first, near, far_odd, relayed(near))

time: 74.4 us -> 71.5 us (0.961)
  Pallas kernels: 46.1 us -> 39.6 us
  waiting for transfers between devices: 16.2 us -> 19.2 us
    pallas_call x2, Pallas kernels: 21.5 us -> 14.9 us  [whiten(): pl.pallas_call(whiten_kernel, grid=(chans // WHITEN_CHANS,), out_shape=ja...]
    ppermute x2, waiting for transfers between devices: 16.2 us -> 19.2 us  [relayed(): return lax.ppermute(near, 'chan', [(i, i - 1) for i in range(1, count, 2)])]
    broadcast_in_dim x0 -> x2, local copies, waits for them, and re-layouts: none -> 1.16 us  [local(): usable = jnp.broadcast_to(usable, (usable.shape[0], LANES))]
  transfers between devices with their start and end apart: 6 -> 6, of which waited for: 2 -> 2; matrix products, arithmetic and copies ran while one was open for 0% -> 0% of each run, Pallas kernels for 24% -> 22%
where the time goes in v4:
time: 71.5 us; the launch traced here: 70.8 us
  Pallas kernels  39.6 us (55%)
  waiting for transfers between devices  19.2 us (27%)
  starting transfers between devices  6.54 us (9%)
  local copies, waits for them, and re-layouts  4.7 us (7%)
    ppermute x2, waiting for transfers between devices, relayed(): return lax.ppermute(near, 'chan', [(i, i - 1) for i in range(1, count, 2)])  19.2 us
    pallas_call x1, Pallas kernels, late_correlate(): pl.pallas_call(kernel, grid=(gram_steps + chans // STEP_CHANS,), out_shap...  16.8 us
    pallas_call x2, Pallas kernels, whiten(): pl.pallas_call(whiten_kernel, grid=(chans // WHITEN_CHANS,), out_shape=ja...  14.9 us
    pallas_call x1, Pallas kernels, early_cross(): pl.pallas_call(early_kernel, grid=(steps,), out_shape=jax.ShapeDtypeStruc...  7.79 us
    unnamed x14, local copies, waits for them, and re-layouts  2.64 us
    ppermute x2, starting transfers between devices, neighbours(): near = lax.ppermute(own, 'chan', [(i, i - 1) for i in range(1, count)])  2.57 us
    ppermute x2, starting transfers between devices, relayed(): return lax.ppermute(near, 'chan', [(i, i - 1) for i in range(1, count, 2)])  2.56 us
  transfers between devices with their start and end apart: 6, of which 2 were waited for; matrix products, arithmetic and copies ran while one was open for 0% of the time, Pallas kernels for 22%

profile of v4, /device:TPU:0, one launch (start us, length us, event | category | flops | bytes accessed | tf_op | source)
XLA Modules:
  0.0 70.8 jit_solution(5280601966837502015)
XLA Ops:
  0.0 0.7 convert_element_type.3
  0.7 0.1 copy.11
  0.8 0.1 broadcast_in_dim.14
  0.9 1.1 %broadcast_in_dim.15.quality_ref = f32[1280,128]{1,0:T(8,128)} broadcast(f32[1280]{0:T(1024)S(1)} %broadcast_in_dim.14), dimensions={0} | broadcast | bytes 660480 | tf_op jit(solution)/shard_map/broadcast_in_dim | solution.py:301
  2.0 7.5 %shard_map.83.own_ref = bf16[80,4096]{1,0:T(8,128)(2,1)} custom-call(bf16[80,16,1500]{2,1,0:T(8,128)(2,1)} %traces_ref.3, f32[1280,128]{1,0:T(8,128)} %broadcast_in_dim.15.quality_ref, bf16[1536,512]{1,0:T(8,128)(2,1)} %constant.8.clone.dft_ref, bf16[256,128]{1,0:T(8,128)(2,1)} %constant.9.clone.band_ref), custom_call_target="tpu_custom_call" | custom-call | flops 1966080000 | bytes 8000000 | tf_op jit(solution)/shard_map/pallas_call | solution.py:108
  9.4 1.3 %collective-permute-start.1 = (bf16[80,4096]{1,0:T(8,128)(2,1)}, bf16[80,4096]{1,0:T(8,128)(2,1)S(1)}, u32[]{:S(2)}, u32[]{:S(2)}) collective-permute-start(bf16[80,4096]{1,0:T(8,128)(2,1)} %shard_map.83.own_ref), channel_id=1, source_target_pairs={{1,0},{2,1},{3,2},{4,3},{5,4},{6,5},{7,6},{8,7},{9,8},{10,9},{11,1... | collective-permute-start | bytes 1966088 | tf_op jit(solution)/shard_map/ppermute | solution.py:288
  10.7 0.7 collective-permute-start.2
  11.4 7.5 %shard_map.82.near_ref.far_ref.refs_1_ = bf16[80,4096]{1,0:T(8,128)(2,1)} custom-call(bf16[80,16,1500]{2,1,0:T(8,128)(2,1)} %traces_ref.3, f32[1280,128]{1,0:T(8,128)} %broadcast_in_dim.15.quality_ref, bf16[1536,512]{1,0:T(8,128)(2,1)} %constant.10.clone.dft_ref, bf16[256,128]{1,0:T(8,128)(2,1)} %constant.9.clone.band_ref), custom_call_target="tpu_custom_call" | custom-call | flops 1966080000 | bytes 8000000 | tf_op jit(solution)/shard_map/pallas_call | solution.py:108
  18.9 0.0 collective-permute-done.1.value_ref
  18.9 0.0 copy-start.1
  18.9 0.8 %copy-done.1 = bf16[80,4096]{1,0:T(8,128)(2,1)} copy-done((bf16[80,4096]{1,0:T(8,128)(2,1)}, bf16[80,4096]{1,0:T(8,128)(2,1)S(1)}, u32[]{:S(2)}) %copy-start.1) | copy-done | bytes 655384
  19.7 1.3 %collective-permute-start.3 = (bf16[80,4096]{1,0:T(8,128)(2,1)}, bf16[80,4096]{1,0:T(8,128)(2,1)S(1)}, u32[]{:S(2)}, u32[]{:S(2)}) collective-permute-start(bf16[80,4096]{1,0:T(8,128)(2,1)} %shard_map.84.near_ref), channel_id=1, source_target_pairs={{1,0},{3,2},{5,4},{7,6},{9,8},{11,10},{13,12},{15,14},{17,16},{19,... | collective-permute-start | bytes 1966088 | tf_op jit(solution)/shard_map/ppermute | solution.py:295
  21.0 0.7 collective-permute-start.4
  21.7 1.3 %collective-permute-start = (bf16[80,4096]{1,0:T(8,128)(2,1)}, bf16[80,4096]{1,0:T(8,128)(2,1)S(1)}, u32[]{:S(2)}, u32[]{:S(2)}) collective-permute-start(bf16[80,4096]{1,0:T(8,128)(2,1)} %shard_map.82.near_ref.far_ref.refs_1_), channel_id=1, source_target_pairs={{1,0},{2,1},{3,2},{4,3},{5,4},{6,5},{7,6},{8,7},{9,8},{10,9},{11,1... | collective-permute-start | bytes 1966088 | tf_op jit(solution)/shard_map/ppermute | solution.py:288
  23.0 0.0 collective-permute-done.2.far_odd_ref
  23.0 0.0 copy-start.4
  23.1 8.9 %collective-permute-done.3.far_even_ref = bf16[80,4096]{1,0:T(8,128)(2,1)S(1)} collective-permute-done((bf16[80,4096]{1,0:T(8,128)(2,1)}, bf16[80,4096]{1,0:T(8,128)(2,1)S(1)}, u32[]{:S(2)}, u32[]{:S(2)}) %collective-permute-start.3) | collective-permute-done | bytes 655392 | tf_op jit(solution)/shard_map/ppermute | solution.py:295
  32.0 0.0 copy-done.4
  32.0 0.0 copy-start.5
  32.0 0.9 %copy-done.5 = bf16[80,4096]{1,0:T(8,128)(2,1)} copy-done((bf16[80,4096]{1,0:T(8,128)(2,1)}, bf16[80,4096]{1,0:T(8,128)(2,1)S(1)}, u32[]{:S(2)}) %copy-start.5) | copy-done | bytes 655384
  32.8 7.8 %shard_map.85.near_ref.far_ref.refs_5_ = bf16[80,256,256]{2,1,0:T(8,128)(2,1)} custom-call(bf16[80,4096]{1,0:T(8,128)(2,1)} %shard_map.83.own_ref, bf16[80,4096]{1,0:T(8,128)(2,1)} %shard_map.84.near_ref, bf16[80,4096]{1,0:T(8,128)(2,1)} %copy-done.4, bf16[80,4096]{1,0:T(8,128)(2,1)} %copy-done.5), custom_call_target="tpu_custom_call" | custom-call | flops 8000000000 | bytes 13000000 | tf_op jit(solution)/shard_map/pallas_call | solution.py:171
  40.6 0.0 copy-start.2
  40.6 0.0 collective-permute-done.value_ref
  40.6 0.0 copy-start
  40.6 0.9 %copy-done = bf16[80,4096]{1,0:T(8,128)(2,1)} copy-done((bf16[80,4096]{1,0:T(8,128)(2,1)}, bf16[80,4096]{1,0:T(8,128)(2,1)S(1)}, u32[]{:S(2)}) %copy-start) | copy-done | bytes 655384
  41.5 1.3 %collective-permute-start.5 = (bf16[80,4096]{1,0:T(8,128)(2,1)}, bf16[80,4096]{1,0:T(8,128)(2,1)S(1)}, u32[]{:S(2)}, u32[]{:S(2)}) collective-permute-start(bf16[80,4096]{1,0:T(8,128)(2,1)} %shard_map.86.refs_2_), channel_id=1, source_target_pairs={{1,0},{3,2},{5,4},{7,6},{9,8},{11,10},{13,12},{15,14},{17,16},{19,... | collective-permute-start | bytes 1966088 | tf_op jit(solution)/shard_map/ppermute | solution.py:295
  42.8 0.0 collective-permute-done.4.refs_3_
  42.8 0.0 copy-start.3
  42.8 10.3 %collective-permute-done.5.refs_4_ = bf16[80,4096]{1,0:T(8,128)(2,1)S(1)} collective-permute-done((bf16[80,4096]{1,0:T(8,128)(2,1)}, bf16[80,4096]{1,0:T(8,128)(2,1)S(1)}, u32[]{:S(2)}, u32[]{:S(2)}) %collective-permute-start.5) | collective-permute-done | bytes 655392 | tf_op jit(solution)/shard_map/ppermute | solution.py:295
  53.1 0.0 copy-done.2
  53.1 0.0 copy-start.6
  53.1 0.8 %broadcast_in_dim.6.refs_0_ = s32[80,128]{1,0:T(8,128)} broadcast(s32[80]{0:T(128)S(1)} %copy-done.2), dimensions={0} | broadcast | bytes 41280 | tf_op jit(solution)/shard_map/broadcast_in_dim | solution.py:261
  53.9 0.0 copy-done.3
  53.9 0.1 copy-done.6
  53.9 16.8 %shard_map.87 = bf16[161,80,201]{2,1,0:T(8,128)(2,1)} custom-call(s32[80,128]{1,0:T(8,128)} %broadcast_in_dim.6.refs_0_, bf16[80,4096]{1,0:T(8,128)(2,1)} %shard_map.82.near_ref.far_ref.refs_1_, bf16[80,4096]{1,0:T(8,128)(2,1)} %shard_map.86.refs_2_, bf16[80,4096]{1,0:T(8,128)(2,1)} %copy-done.3, bf16[80,4096]{1,0:T(8,128)(2,1)} %copy-done.6, ...), custom_call_target="tpu_custom_call" | custom-call | flops 12000000000 | bytes 20000000 | tf_op jit(solution)/shard_map/pallas_call | solution.py:243
  (2 shorter events, 0.0 us)
Async XLA Ops:
  9.4 9.5 %collective-permute-start.1 = (bf16[80,4096]{1,0:T(8,128)(2,1)}, bf16[80,4096]{1,0:T(8,128)(2,1)S(1)}, u32[]{:S(2)}, u32[]{:S(2)}) collective-permute-start(bf16[80,4096]{1,0:T(8,128)(2,1)} %shard_map.83.own_ref), channel_id=1, source_target_pairs={{1,0},{2,1},{3,2},{4,3},{5,4},{6,5},{7,6},{8,7},{9,8},{10,9},{11,1... | collective-permute-start | bytes 1966088 | tf_op jit(solution)/shard_map/ppermute | solution.py:288
  10.7 12.3 %collective-permute-start.2 = (bf16[80,4096]{1,0:T(8,128)(2,1)}, bf16[80,4096]{1,0:T(8,128)(2,1)S(1)}, u32[]{:S(2)}, u32[]{:S(2)}) collective-permute-start(bf16[80,4096]{1,0:T(8,128)(2,1)} %shard_map.83.own_ref), channel_id=1, source_target_pairs={{3,1},{5,3},{7,5},{9,7},{11,9},{13,11},{15,13},{19,17},{21,19},{23... | collective-permute-start | bytes 1966088 | tf_op jit(solution)/shard_map/ppermute | solution.py:289
  18.9 0.8 %copy-start.1 = (bf16[80,4096]{1,0:T(8,128)(2,1)}, bf16[80,4096]{1,0:T(8,128)(2,1)S(1)}, u32[]{:S(2)}) copy-start(bf16[80,4096]{1,0:T(8,128)(2,1)S(1)} %collective-permute-done.1.value_ref) | copy-start | bytes 1966084
  19.7 12.2 %collective-permute-start.3 = (bf16[80,4096]{1,0:T(8,128)(2,1)}, bf16[80,4096]{1,0:T(8,128)(2,1)S(1)}, u32[]{:S(2)}, u32[]{:S(2)}) collective-permute-start(bf16[80,4096]{1,0:T(8,128)(2,1)} %shard_map.84.near_ref), channel_id=1, source_target_pairs={{1,0},{3,2},{5,4},{7,6},{9,8},{11,10},{13,12},{15,14},{17,16},{19,... | collective-permute-start | bytes 1966088 | tf_op jit(solution)/shard_map/ppermute | solution.py:295
  21.0 21.8 %collective-permute-start.4 = (bf16[80,4096]{1,0:T(8,128)(2,1)}, bf16[80,4096]{1,0:T(8,128)(2,1)S(1)}, u32[]{:S(2)}, u32[]{:S(2)}) collective-permute-start(bf16[80,4096]{1,0:T(8,128)(2,1)} %shard_map.82.near_ref.far_ref.refs_1_), channel_id=1, source_target_pairs={{3,1},{5,3},{7,5},{9,7},{11,9},{13,11},{15,13},{19,17},{21,19},{23... | collective-permute-start | bytes 1966088 | tf_op jit(solution)/shard_map/ppermute | solution.py:289
  21.7 18.9 %collective-permute-start = (bf16[80,4096]{1,0:T(8,128)(2,1)}, bf16[80,4096]{1,0:T(8,128)(2,1)S(1)}, u32[]{:S(2)}, u32[]{:S(2)}) collective-permute-start(bf16[80,4096]{1,0:T(8,128)(2,1)} %shard_map.82.near_ref.far_ref.refs_1_), channel_id=1, source_target_pairs={{1,0},{2,1},{3,2},{4,3},{5,4},{6,5},{7,6},{8,7},{9,8},{10,9},{11,1... | collective-permute-start | bytes 1966088 | tf_op jit(solution)/shard_map/ppermute | solution.py:288
  23.0 8.9 %copy-start.4 = (bf16[80,4096]{1,0:T(8,128)(2,1)}, bf16[80,4096]{1,0:T(8,128)(2,1)S(1)}, u32[]{:S(2)}) copy-start(bf16[80,4096]{1,0:T(8,128)(2,1)S(1)} %collective-permute-done.2.far_odd_ref) | copy-start | bytes 1966084
  32.0 0.9 %copy-start.5 = (bf16[80,4096]{1,0:T(8,128)(2,1)}, bf16[80,4096]{1,0:T(8,128)(2,1)S(1)}, u32[]{:S(2)}) copy-start(bf16[80,4096]{1,0:T(8,128)(2,1)S(1)} %collective-permute-done.3.far_even_ref) | copy-start | bytes 1966084
  40.6 12.4 %copy-start.2 = (s32[80]{0:T(128)S(1)}, s32[80]{0:T(128)}, u32[]{:S(2)}) copy-start(s32[80]{0:T(128)} %param.10) | copy-start | bytes 964
  40.6 0.9 %copy-start = (bf16[80,4096]{1,0:T(8,128)(2,1)}, bf16[80,4096]{1,0:T(8,128)(2,1)S(1)}, u32[]{:S(2)}) copy-start(bf16[80,4096]{1,0:T(8,128)(2,1)S(1)} %collective-permute-done.value_ref) | copy-start | bytes 1966084
  41.5 11.6 %collective-permute-start.5 = (bf16[80,4096]{1,0:T(8,128)(2,1)}, bf16[80,4096]{1,0:T(8,128)(2,1)S(1)}, u32[]{:S(2)}, u32[]{:S(2)}) collective-permute-start(bf16[80,4096]{1,0:T(8,128)(2,1)} %shard_map.86.refs_2_), channel_id=1, source_target_pairs={{1,0},{3,2},{5,4},{7,6},{9,8},{11,10},{13,12},{15,14},{17,16},{19,... | collective-permute-start | bytes 1966088 | tf_op jit(solution)/shard_map/ppermute | solution.py:295
  42.8 11.1 %copy-start.3 = (bf16[80,4096]{1,0:T(8,128)(2,1)}, bf16[80,4096]{1,0:T(8,128)(2,1)S(1)}, u32[]{:S(2)}) copy-start(bf16[80,4096]{1,0:T(8,128)(2,1)S(1)} %collective-permute-done.4.refs_3_) | copy-start | bytes 1966084
  53.1 0.9 %copy-start.6 = (bf16[80,4096]{1,0:T(8,128)(2,1)}, bf16[80,4096]{1,0:T(8,128)(2,1)S(1)}, u32[]{:S(2)}) copy-start(bf16[80,4096]{1,0:T(8,128)(2,1)S(1)} %collective-permute-done.5.refs_4_) | copy-start | bytes 1966084

commit v5 on v4

--- a/solution.py
+++ b/solution.py
@@ -14,6 +14,7 @@
 HALF_SMOOTH = 32
 LAG = 100
 LAGS = 2 * LAG + 1
+LAG_ROWS = -(-LAGS // 16) * 16
 LANES = 128
 PIECES = -(-S // LANES)
 GROUP = 8
@@ -60,7 +61,7 @@
     both = both.reshape(LAGS, 2, GROUPS, GROUP).transpose(0, 2, 1, 3).reshape(LAGS, 2 * F)
     scale = np.float32(1.0 / (windows * math.sqrt(F)))
     both = (both.astype(np.float32) * scale).astype(jnp.bfloat16)
-    return np.concatenate([both, np.zeros((256 - LAGS, 2 * F), jnp.bfloat16)], axis=0)
+    return np.concatenate([both, np.zeros((LAG_ROWS - LAGS, 2 * F), jnp.bfloat16)], axis=0)
 
 
 def whiten_kernel(traces_ref, quality_ref, dft_ref, band_ref, out_ref, wide):
@@ -79,7 +80,13 @@
     low = (amplitude - high.astype(jnp.float32)).astype(jnp.bfloat16)
     smooth = jnp.dot(high, band_ref[...], preferred_element_type=jnp.float32)
     smooth = smooth + jnp.dot(low, band_ref[...], preferred_element_type=jnp.float32)
-    scale = quality_ref[...] / (smooth * (1.0 / (2 * HALF_SMOOTH + 1)) + eps)
+    lane = lax.broadcasted_iota(jnp.int32, quality_ref.shape, 1) - pl.program_id(0) * chans
+    quality = quality_ref[...].astype(jnp.float32)
+    usable = [
+        jnp.sum(jnp.where(lane == c, quality, 0.0), axis=1, keepdims=True) for c in range(chans)
+    ]
+    usable = jnp.concatenate([jnp.broadcast_to(u, (windows, LANES)) for u in usable], axis=0)
+    scale = usable / (smooth * (1.0 / (2 * HALF_SMOOTH + 1)) + eps)
     place = lax.broadcasted_iota(jnp.int32, (chans, LANES), 1) // GROUP
     for i in range(2):
         value = own[i] * scale
@@ -101,7 +108,7 @@
             out_ref[:, start : start + LANES] = turned[g].astype(jnp.bfloat16)
 
 
-def whiten(traces, usable, first):
+def whiten(traces, quality, first):
     chans, windows, _ = traces.shape
     columns = 2 * LANES * windows
     whole = pl.BlockSpec(memory_space=pltpu.VMEM)
@@ -111,7 +118,7 @@
         out_shape=jax.ShapeDtypeStruct((chans, columns), jnp.bfloat16),
         in_specs=[
             pl.BlockSpec((WHITEN_CHANS, windows, S), lambda i: (i, 0, 0)),
-            pl.BlockSpec((WHITEN_CHANS * windows, LANES), lambda i: (i, 0)),
+            whole,
             whole,
             whole,
         ],
@@ -121,16 +128,16 @@
         cost_estimate=pl.CostEstimate(
             flops=8 * chans * windows * S * LANES, bytes_accessed=8_000_000, transcendentals=0
         ),
-    )(traces, usable, jnp.asarray(dft_columns(first)), jnp.asarray(band_columns()))
-
-
-def gram(own_ref, near_ref, far_odd_ref, far_even_ref, store):
+    )(traces, quality.T, jnp.asarray(dft_columns(first)), jnp.asarray(band_columns()))
+
+
+def gram(own_ref, near_ref, far_odd_ref, far_even_ref, wide, store):
     chans = own_ref.shape[0]
     depth = own_ref.shape[1] // STEP_GROUPS
     half = depth // 2
     spot = lax.broadcasted_iota(jnp.int32, (GROUP, half), 1) % GROUP
     row = lax.broadcasted_iota(jnp.int32, (GROUP, half), 0)
-    mask = (spot == row)[None]
+    mask = spot == row
     for g in range(STEP_GROUPS):
         columns = slice(g * depth, (g + 1) * depth)
         own = own_ref[:, columns]
@@ -138,17 +145,19 @@
         fill = jnp.zeros((SPAN - 3 * chans, depth), jnp.bfloat16)
         others = jnp.concatenate([own, near_ref[:, columns], far, fill], axis=0)
         value = own.astype(jnp.float32)
-        real = jnp.where(mask, value[:, None, :half], 0.0)
-        imag = jnp.where(mask, value[:, None, half:], 0.0)
-        left = jnp.concatenate(
-            [
-                jnp.concatenate([real, imag], axis=2),
-                jnp.concatenate([imag, -real], axis=2),
-            ],
-            axis=1,
-        ).astype(jnp.bfloat16)
+        wide[2 * g] = value[:, :half]
+        wide[2 * g + 1] = value[:, half:]
+        left = []
+        for c in range(chans):
+            real = jnp.broadcast_to(wide[2 * g, c : c + 1, :], (GROUP, half))
+            imag = jnp.broadcast_to(wide[2 * g + 1, c : c + 1, :], (GROUP, half))
+            real = jnp.where(mask, real, 0.0)
+            imag = jnp.where(mask, imag, 0.0)
+            upper = jnp.concatenate([real, imag], axis=0).astype(jnp.bfloat16)
+            lower = jnp.concatenate([imag, -real], axis=0).astype(jnp.bfloat16)
+            left.append(jnp.concatenate([upper, lower], axis=1))
         products = lax.dot_general(
-            left.reshape(chans * 2 * GROUP, depth),
+            jnp.concatenate(left, axis=0),
             others,
             (((1,), (1,)), ((), ())),
             preferred_element_type=jnp.float32,
@@ -156,11 +165,11 @@
         store(g, products.astype(jnp.bfloat16).reshape(chans, 2 * GROUP, SPAN))
 
 
-def early_kernel(own_ref, near_ref, far_odd_ref, far_even_ref, cross_ref):
+def early_kernel(own_ref, near_ref, far_odd_ref, far_even_ref, cross_ref, wide):
     def store(g, products):
         cross_ref[:, g * 2 * GROUP : (g + 1) * 2 * GROUP, :] = products
 
-    gram(own_ref, near_ref, far_odd_ref, far_even_ref, store)
+    gram(own_ref, near_ref, far_odd_ref, far_even_ref, wide, store)
 
 
 def early_cross(own, near, far_odd, far_even):
@@ -174,6 +183,7 @@
         out_shape=jax.ShapeDtypeStruct((chans, steps * rows, SPAN), jnp.bfloat16),
         in_specs=[block] * 4,
         out_specs=pl.BlockSpec((chans, rows, SPAN), lambda i: (0, i, 0)),
+        scratch_shapes=[pltpu.VMEM((2 * STEP_GROUPS, chans, LANES), jnp.float32)],
         compiler_params=pltpu.CompilerParams(vmem_limit_bytes=VMEM_LIMIT),
         cost_estimate=pl.CostEstimate(
             flops=8_000_000_000, bytes_accessed=13_000_000, transcendentals=0
@@ -193,6 +203,7 @@
     out_ref,
     cross,
     turned,
+    wide,
 ):
     chans = own_ref.shape[0]
     step = pl.program_id(0)
@@ -203,7 +214,7 @@
             start = pl.multiple_of((step * STEP_GROUPS + g) * 2 * GROUP, 2 * GROUP)
             cross[:, pl.ds(start, 2 * GROUP), :] = products
 
-        gram(own_ref, near_ref, far_odd_ref, far_even_ref, store)
+        gram(own_ref, near_ref, far_odd_ref, far_even_ref, wide, store)
 
     @pl.when(step >= gram_steps)
     def _():
@@ -218,8 +229,14 @@
             start = (chans - c) * PITCH + j
             for p in range(2):
                 part = lagged[p * LANES : (p + 1) * LANES].T
+                if part.shape[1] < LANES:
+                    rest = jnp.zeros((SPAN, LANES - part.shape[1]), jnp.float32)
+                    part = jnp.concatenate([part, rest], axis=1)
                 turned[p, pl.ds(start, SPAN, stride=PITCH), :] = part
-        reach = reach_ref[...]
+        row = lax.broadcasted_iota(jnp.int32, (STEP_CHANS, LANES), 0)
+        reach = jnp.zeros((STEP_CHANS, LANES), jnp.int32)
+        for j in range(STEP_CHANS):
+            reach = jnp.where(row == j, reach_ref[base + j], reach)
         for k in range(R + 1):
             start = (chans + k) * PITCH
             for p in range(2):
@@ -244,7 +261,7 @@
         kernel,
         grid=(gram_steps + chans // STEP_CHANS,),
         out_shape=jax.ShapeDtypeStruct((R + 1, chans, LAGS), jnp.bfloat16),
-        in_specs=[pl.BlockSpec((STEP_CHANS, LANES), lambda i: (later(i), 0))]
+        in_specs=[pl.BlockSpec(memory_space=pltpu.SMEM)]
         + [block] * 4
         + [pl.BlockSpec((STEP_CHANS, depth, SPAN), lambda i: (later(i), 0, 0))]
         + [pl.BlockSpec(memory_space=pltpu.VMEM)],
@@ -252,13 +269,14 @@
         scratch_shapes=[
             pltpu.VMEM((chans, 2 * F - depth, SPAN), jnp.bfloat16),
             pltpu.VMEM((2, (chans + SPAN) * PITCH, LANES), jnp.float32),
+            pltpu.VMEM((2 * STEP_GROUPS, chans, LANES), jnp.float32),
         ],
         compiler_params=pltpu.CompilerParams(vmem_limit_bytes=VMEM_LIMIT),
         cost_estimate=pl.CostEstimate(
             flops=12_000_000_000, bytes_accessed=20_000_000, transcendentals=0
         ),
     )(
-        jnp.broadcast_to(reach[:, None], (chans, LANES)),
+        reach,
         own,
         near,
         far_odd,
@@ -297,11 +315,9 @@
 
 def local(traces, quality, reach):
     windows = traces.shape[1]
-    usable = quality.astype(jnp.float32).reshape(-1, 1)
-    usable = jnp.broadcast_to(usable, (usable.shape[0], LANES))
-    first = whiten(traces, usable, 0)
+    first = whiten(traces, quality, 0)
     near, far_odd = neighbours(first)
-    second = whiten(traces, usable, LANES)
+    second = whiten(traces, quality, LANES)
     next_near, next_odd = neighbours(second)
     near = follow(near, second, second)
     early = early_cross(first, near, far_odd, relayed(near))

time: 71.5 us -> 69.5 us (0.972)
  local copies, waits for them, and re-layouts: 4.7 us -> 3.44 us
    broadcast_in_dim x3 -> x0, local copies, waits for them, and re-layouts: 1.96 us -> none  [the longest x2 1.16 us: local(): usable = jnp.broadcast_to(usable, (usable.shape[0], LANES))]
    unnamed x14 -> x12, local copies, waits for them, and re-layouts: 2.64 us -> 3.44 us
where the time goes in v5:
time: 69.5 us; the launch traced here: 68.8 us
  Pallas kernels  39.4 us (57%)
  waiting for transfers between devices  19.4 us (28%)
  starting transfers between devices  6.54 us (9%)
  local copies, waits for them, and re-layouts  3.44 us (5%)
    ppermute x2, waiting for transfers between devices, relayed(): return lax.ppermute(near, 'chan', [(i, i - 1) for i in range(1, count, 2)])  19.3 us
    pallas_call x1, Pallas kernels, late_correlate(): pl.pallas_call(kernel, grid=(gram_steps + chans // STEP_CHANS,), out_shap...  16.8 us
    pallas_call x2, Pallas kernels, whiten(): pl.pallas_call(whiten_kernel, grid=(chans // WHITEN_CHANS,), out_shape=ja...  14.8 us
    pallas_call x1, Pallas kernels, early_cross(): pl.pallas_call(early_kernel, grid=(steps,), out_shape=jax.ShapeDtypeStruc...  7.68 us
    unnamed x12, local copies, waits for them, and re-layouts  3.44 us
    ppermute x2, starting transfers between devices, neighbours(): near = lax.ppermute(own, 'chan', [(i, i - 1) for i in range(1, count)])  2.57 us
    ppermute x2, starting transfers between devices, relayed(): return lax.ppermute(near, 'chan', [(i, i - 1) for i in range(1, count, 2)])  2.56 us
    ppermute x2, starting transfers between devices, neighbours(): lax.ppermute(own, 'chan', [(i, i - 2) for i in range(3, count, 2)])  1.41 us
  transfers between devices with their start and end apart: 6, of which 2 were waited for; matrix products, arithmetic and copies ran while one was open for 0% of the time, Pallas kernels for 22%

profile of v5, /device:TPU:0, one launch (start us, length us, event | category | flops | bytes accessed | tf_op | source)
XLA Modules:
  0.0 68.8 jit_solution(3608597029885250444)
XLA Ops:
  0.0 7.4 %shard_map.83.own_ref = bf16[80,4096]{1,0:T(8,128)(2,1)} custom-call(bf16[80,16,1500]{2,1,0:T(8,128)(2,1)} %traces_ref.3, s32[16,80]{1,0:T(8,128)} %bitcast.2, bf16[1536,512]{1,0:T(8,128)(2,1)} %constant.8.clone.dft_ref, bf16[256,128]{1,0:T(8,128)(2,1)} %constant.9.clone.band_ref), custom_call_target="tpu_custom_call" | custom-call | flops 1966080000 | bytes 8000000 | tf_op jit(solution)/shard_map/pallas_call | solution.py:115
  7.4 1.3 %collective-permute-start.1 = (bf16[80,4096]{1,0:T(8,128)(2,1)}, bf16[80,4096]{1,0:T(8,128)(2,1)S(1)}, u32[]{:S(2)}, u32[]{:S(2)}) collective-permute-start(bf16[80,4096]{1,0:T(8,128)(2,1)} %shard_map.83.own_ref), channel_id=1, source_target_pairs={{1,0},{2,1},{3,2},{4,3},{5,4},{6,5},{7,6},{8,7},{9,8},{10,9},{11,1... | collective-permute-start | bytes 1966088 | tf_op jit(solution)/shard_map/ppermute | solution.py:306
  8.7 0.7 %collective-permute-start.2 = (bf16[80,4096]{1,0:T(8,128)(2,1)}, bf16[80,4096]{1,0:T(8,128)(2,1)S(1)}, u32[]{:S(2)}, u32[]{:S(2)}) collective-permute-start(bf16[80,4096]{1,0:T(8,128)(2,1)} %shard_map.83.own_ref), channel_id=1, source_target_pairs={{3,1},{5,3},{7,5},{9,7},{11,9},{13,11},{15,13},{19,17},{21,19},{23... | collective-permute-start | bytes 1966088 | tf_op jit(solution)/shard_map/ppermute | solution.py:307
  9.4 7.4 %shard_map.82.near_ref.far_ref.refs_1_ = bf16[80,4096]{1,0:T(8,128)(2,1)} custom-call(bf16[80,16,1500]{2,1,0:T(8,128)(2,1)} %traces_ref.3, s32[16,80]{1,0:T(8,128)} %bitcast.3, bf16[1536,512]{1,0:T(8,128)(2,1)} %constant.10.clone.dft_ref, bf16[256,128]{1,0:T(8,128)(2,1)} %constant.9.clone.band_ref), custom_call_target="tpu_custom_call" | custom-call | flops 1966080000 | bytes 8000000 | tf_op jit(solution)/shard_map/pallas_call | solution.py:115
  16.8 0.0 collective-permute-done.1.value_ref
  16.8 0.0 copy-start.1
  16.8 0.9 %copy-done.1 = bf16[80,4096]{1,0:T(8,128)(2,1)} copy-done((bf16[80,4096]{1,0:T(8,128)(2,1)}, bf16[80,4096]{1,0:T(8,128)(2,1)S(1)}, u32[]{:S(2)}) %copy-start.1) | copy-done | bytes 655384
  17.7 1.3 %collective-permute-start.3 = (bf16[80,4096]{1,0:T(8,128)(2,1)}, bf16[80,4096]{1,0:T(8,128)(2,1)S(1)}, u32[]{:S(2)}, u32[]{:S(2)}) collective-permute-start(bf16[80,4096]{1,0:T(8,128)(2,1)} %shard_map.84.near_ref), channel_id=1, source_target_pairs={{1,0},{3,2},{5,4},{7,6},{9,8},{11,10},{13,12},{15,14},{17,16},{19,... | collective-permute-start | bytes 1966088 | tf_op jit(solution)/shard_map/ppermute | solution.py:313
  19.0 0.7 %collective-permute-start.4 = (bf16[80,4096]{1,0:T(8,128)(2,1)}, bf16[80,4096]{1,0:T(8,128)(2,1)S(1)}, u32[]{:S(2)}, u32[]{:S(2)}) collective-permute-start(bf16[80,4096]{1,0:T(8,128)(2,1)} %shard_map.82.near_ref.far_ref.refs_1_), channel_id=1, source_target_pairs={{3,1},{5,3},{7,5},{9,7},{11,9},{13,11},{15,13},{19,17},{21,19},{23... | collective-permute-start | bytes 1966088 | tf_op jit(solution)/shard_map/ppermute | solution.py:307
  19.7 1.3 %collective-permute-start = (bf16[80,4096]{1,0:T(8,128)(2,1)}, bf16[80,4096]{1,0:T(8,128)(2,1)S(1)}, u32[]{:S(2)}, u32[]{:S(2)}) collective-permute-start(bf16[80,4096]{1,0:T(8,128)(2,1)} %shard_map.82.near_ref.far_ref.refs_1_), channel_id=1, source_target_pairs={{1,0},{2,1},{3,2},{4,3},{5,4},{6,5},{7,6},{8,7},{9,8},{10,9},{11,1... | collective-permute-start | bytes 1966088 | tf_op jit(solution)/shard_map/ppermute | solution.py:306
  21.0 0.0 collective-permute-done.2.far_odd_ref
  21.0 0.0 copy-start.3
  21.0 9.0 %collective-permute-done.3.far_even_ref = bf16[80,4096]{1,0:T(8,128)(2,1)S(1)} collective-permute-done((bf16[80,4096]{1,0:T(8,128)(2,1)}, bf16[80,4096]{1,0:T(8,128)(2,1)S(1)}, u32[]{:S(2)}, u32[]{:S(2)}) %collective-permute-start.3) | collective-permute-done | bytes 655392 | tf_op jit(solution)/shard_map/ppermute | solution.py:313
  30.0 0.0 copy-done.3
  30.0 0.0 copy-start.4
  30.0 0.8 %copy-done.4 = bf16[80,4096]{1,0:T(8,128)(2,1)} copy-done((bf16[80,4096]{1,0:T(8,128)(2,1)}, bf16[80,4096]{1,0:T(8,128)(2,1)S(1)}, u32[]{:S(2)}) %copy-start.4) | copy-done | bytes 655384
  30.8 7.7 %shard_map.85.near_ref.far_ref.refs_5_ = bf16[80,256,256]{2,1,0:T(8,128)(2,1)} custom-call(bf16[80,4096]{1,0:T(8,128)(2,1)} %shard_map.83.own_ref, bf16[80,4096]{1,0:T(8,128)(2,1)} %shard_map.84.near_ref, bf16[80,4096]{1,0:T(8,128)(2,1)} %copy-done.3, bf16[80,4096]{1,0:T(8,128)(2,1)} %copy-done.4), custom_call_target="tpu_custom_call" | custom-call | flops 8000000000 | bytes 13000000 | tf_op jit(solution)/shard_map/pallas_call | solution.py:180
  38.5 0.0 collective-permute-done.value_ref
  38.5 0.0 copy-start
  38.5 0.9 %copy-done = bf16[80,4096]{1,0:T(8,128)(2,1)} copy-done((bf16[80,4096]{1,0:T(8,128)(2,1)}, bf16[80,4096]{1,0:T(8,128)(2,1)S(1)}, u32[]{:S(2)}) %copy-start) | copy-done | bytes 655384
  39.4 1.3 %collective-permute-start.5 = (bf16[80,4096]{1,0:T(8,128)(2,1)}, bf16[80,4096]{1,0:T(8,128)(2,1)S(1)}, u32[]{:S(2)}, u32[]{:S(2)}) collective-permute-start(bf16[80,4096]{1,0:T(8,128)(2,1)} %shard_map.86.refs_2_), channel_id=1, source_target_pairs={{1,0},{3,2},{5,4},{7,6},{9,8},{11,10},{13,12},{15,14},{17,16},{19,... | collective-permute-start | bytes 1966088 | tf_op jit(solution)/shard_map/ppermute | solution.py:313
  40.7 0.0 collective-permute-done.4.refs_3_
  40.7 0.0 copy-start.2
  40.7 10.4 %collective-permute-done.5.refs_4_ = bf16[80,4096]{1,0:T(8,128)(2,1)S(1)} collective-permute-done((bf16[80,4096]{1,0:T(8,128)(2,1)}, bf16[80,4096]{1,0:T(8,128)(2,1)S(1)}, u32[]{:S(2)}, u32[]{:S(2)}) %collective-permute-start.5) | collective-permute-done | bytes 655392 | tf_op jit(solution)/shard_map/ppermute | solution.py:313
  51.1 0.0 copy-done.2
  51.1 0.0 copy-start.5
  51.1 0.8 %copy-done.5 = bf16[80,4096]{1,0:T(8,128)(2,1)} copy-done((bf16[80,4096]{1,0:T(8,128)(2,1)}, bf16[80,4096]{1,0:T(8,128)(2,1)S(1)}, u32[]{:S(2)}) %copy-start.5) | copy-done | bytes 655384
  51.9 16.8 %shard_map.87 = bf16[161,80,201]{2,1,0:T(8,128)(2,1)} custom-call(s32[80]{0:T(128)} %refs_0_.1, bf16[80,4096]{1,0:T(8,128)(2,1)} %shard_map.82.near_ref.far_ref.refs_1_, bf16[80,4096]{1,0:T(8,128)(2,1)} %shard_map.86.refs_2_, bf16[80,4096]{1,0:T(8,128)(2,1)} %copy-done.2, bf16[80,4096]{1,0:T(8,128)(2,1)} %copy-done.5, ...), custom_call_target="tpu_custom_call" | custom-call | flops 12000000000 | bytes 20000000 | tf_op jit(solution)/shard_map/pallas_call | solution.py:260
  (2 shorter events, 0.0 us)
Async XLA Ops:
  7.4 9.4 %collective-permute-start.1 = (bf16[80,4096]{1,0:T(8,128)(2,1)}, bf16[80,4096]{1,0:T(8,128)(2,1)S(1)}, u32[]{:S(2)}, u32[]{:S(2)}) collective-permute-start(bf16[80,4096]{1,0:T(8,128)(2,1)} %shard_map.83.own_ref), channel_id=1, source_target_pairs={{1,0},{2,1},{3,2},{4,3},{5,4},{6,5},{7,6},{8,7},{9,8},{10,9},{11,1... | collective-permute-start | bytes 1966088 | tf_op jit(solution)/shard_map/ppermute | solution.py:306
  8.7 12.3 %collective-permute-start.2 = (bf16[80,4096]{1,0:T(8,128)(2,1)}, bf16[80,4096]{1,0:T(8,128)(2,1)S(1)}, u32[]{:S(2)}, u32[]{:S(2)}) collective-permute-start(bf16[80,4096]{1,0:T(8,128)(2,1)} %shard_map.83.own_ref), channel_id=1, source_target_pairs={{3,1},{5,3},{7,5},{9,7},{11,9},{13,11},{15,13},{19,17},{21,19},{23... | collective-permute-start | bytes 1966088 | tf_op jit(solution)/shard_map/ppermute | solution.py:307
  16.8 0.9 %copy-start.1 = (bf16[80,4096]{1,0:T(8,128)(2,1)}, bf16[80,4096]{1,0:T(8,128)(2,1)S(1)}, u32[]{:S(2)}) copy-start(bf16[80,4096]{1,0:T(8,128)(2,1)S(1)} %collective-permute-done.1.value_ref) | copy-start | bytes 1966084
  17.7 12.3 %collective-permute-start.3 = (bf16[80,4096]{1,0:T(8,128)(2,1)}, bf16[80,4096]{1,0:T(8,128)(2,1)S(1)}, u32[]{:S(2)}, u32[]{:S(2)}) collective-permute-start(bf16[80,4096]{1,0:T(8,128)(2,1)} %shard_map.84.near_ref), channel_id=1, source_target_pairs={{1,0},{3,2},{5,4},{7,6},{9,8},{11,10},{13,12},{15,14},{17,16},{19,... | collective-permute-start | bytes 1966088 | tf_op jit(solution)/shard_map/ppermute | solution.py:313
  19.0 21.7 %collective-permute-start.4 = (bf16[80,4096]{1,0:T(8,128)(2,1)}, bf16[80,4096]{1,0:T(8,128)(2,1)S(1)}, u32[]{:S(2)}, u32[]{:S(2)}) collective-permute-start(bf16[80,4096]{1,0:T(8,128)(2,1)} %shard_map.82.near_ref.far_ref.refs_1_), channel_id=1, source_target_pairs={{3,1},{5,3},{7,5},{9,7},{11,9},{13,11},{15,13},{19,17},{21,19},{23... | collective-permute-start | bytes 1966088 | tf_op jit(solution)/shard_map/ppermute | solution.py:307
  19.7 18.8 %collective-permute-start = (bf16[80,4096]{1,0:T(8,128)(2,1)}, bf16[80,4096]{1,0:T(8,128)(2,1)S(1)}, u32[]{:S(2)}, u32[]{:S(2)}) collective-permute-start(bf16[80,4096]{1,0:T(8,128)(2,1)} %shard_map.82.near_ref.far_ref.refs_1_), channel_id=1, source_target_pairs={{1,0},{2,1},{3,2},{4,3},{5,4},{6,5},{7,6},{8,7},{9,8},{10,9},{11,1... | collective-permute-start | bytes 1966088 | tf_op jit(solution)/shard_map/ppermute | solution.py:306
  21.0 9.0 %copy-start.3 = (bf16[80,4096]{1,0:T(8,128)(2,1)}, bf16[80,4096]{1,0:T(8,128)(2,1)S(1)}, u32[]{:S(2)}) copy-start(bf16[80,4096]{1,0:T(8,128)(2,1)S(1)} %collective-permute-done.2.far_odd_ref) | copy-start | bytes 1966084
  30.0 0.8 %copy-start.4 = (bf16[80,4096]{1,0:T(8,128)(2,1)}, bf16[80,4096]{1,0:T(8,128)(2,1)S(1)}, u32[]{:S(2)}) copy-start(bf16[80,4096]{1,0:T(8,128)(2,1)S(1)} %collective-permute-done.3.far_even_ref) | copy-start | bytes 1966084
  38.5 0.9 %copy-start = (bf16[80,4096]{1,0:T(8,128)(2,1)}, bf16[80,4096]{1,0:T(8,128)(2,1)S(1)}, u32[]{:S(2)}) copy-start(bf16[80,4096]{1,0:T(8,128)(2,1)S(1)} %collective-permute-done.value_ref) | copy-start | bytes 1966084
  39.4 11.7 %collective-permute-start.5 = (bf16[80,4096]{1,0:T(8,128)(2,1)}, bf16[80,4096]{1,0:T(8,128)(2,1)S(1)}, u32[]{:S(2)}, u32[]{:S(2)}) collective-permute-start(bf16[80,4096]{1,0:T(8,128)(2,1)} %shard_map.86.refs_2_), channel_id=1, source_target_pairs={{1,0},{3,2},{5,4},{7,6},{9,8},{11,10},{13,12},{15,14},{17,16},{19,... | collective-permute-start | bytes 1966088 | tf_op jit(solution)/shard_map/ppermute | solution.py:313
  40.7 10.4 %copy-start.2 = (bf16[80,4096]{1,0:T(8,128)(2,1)}, bf16[80,4096]{1,0:T(8,128)(2,1)S(1)}, u32[]{:S(2)}) copy-start(bf16[80,4096]{1,0:T(8,128)(2,1)S(1)} %collective-permute-done.4.refs_3_) | copy-start | bytes 1966084
  51.1 0.8 %copy-start.5 = (bf16[80,4096]{1,0:T(8,128)(2,1)}, bf16[80,4096]{1,0:T(8,128)(2,1)S(1)}, u32[]{:S(2)}) copy-start(bf16[80,4096]{1,0:T(8,128)(2,1)S(1)} %collective-permute-done.5.refs_4_) | copy-start | bytes 1966084

commit v6 on v5

--- a/solution.py
+++ b/solution.py
@@ -25,7 +25,8 @@
 PITCH = STEP_CHANS + 1
 COLUMNS = 1024
 WHITEN_CHANS = 16
-VMEM_LIMIT = 56 * 1024 * 1024
+VMEM_LIMIT = 32 * 1024 * 1024
+WHITEN_VMEM = 56 * 1024 * 1024
 
 eps = 1e-06
 
@@ -124,7 +125,7 @@
         ],
         out_specs=pl.BlockSpec((WHITEN_CHANS, columns), lambda i: (i, 0)),
         scratch_shapes=[pltpu.VMEM((2, WHITEN_CHANS * (windows + 1), LANES), jnp.float32)],
-        compiler_params=pltpu.CompilerParams(vmem_limit_bytes=VMEM_LIMIT),
+        compiler_params=pltpu.CompilerParams(vmem_limit_bytes=WHITEN_VMEM),
         cost_estimate=pl.CostEstimate(
             flops=8 * chans * windows * S * LANES, bytes_accessed=8_000_000, transcendentals=0
         ),

time: 69.5 us -> 71.7 us (1.032)
  local copies, waits for them, and re-layouts: 3.44 us -> 11.8 us
  Pallas kernels: 39.4 us -> 34.2 us
  waiting for transfers between devices: 19.4 us -> 18.4 us
    unnamed x12 -> x20, local copies, waits for them, and re-layouts: 3.44 us -> 11.8 us
    pallas_call x1, Pallas kernels: 7.68 us -> 4.4 us  [early_cross(): pl.pallas_call(early_kernel, grid=(steps,), out_shape=jax.ShapeDtypeStruc...]
    pallas_call x1, Pallas kernels: 16.8 us -> 14.9 us  [late_correlate(): pl.pallas_call(kernel, grid=(gram_steps + chans // STEP_CHANS,), out_shap...]
    ppermute x2, waiting for transfers between devices: 19.3 us -> 18.4 us  [relayed(): return lax.ppermute(near, 'chan', [(i, i - 1) for i in range(1, count, 2)])]
  transfers between devices with their start and end apart: 6 -> 6, of which waited for: 2 -> 2; matrix products, arithmetic and copies ran while one was open for 0% -> 0% of each run, Pallas kernels for 22% -> 17%
where the time goes in v6:
time: 71.7 us; the launch traced here: 71.2 us
  Pallas kernels  34.2 us (48%)
  waiting for transfers between devices  18.4 us (26%)
  local copies, waits for them, and re-layouts  11.8 us (16%)
  starting transfers between devices  6.67 us (9%)
    ppermute x2, waiting for transfers between devices, relayed(): return lax.ppermute(near, 'chan', [(i, i - 1) for i in range(1, count, 2)])  18.4 us
    pallas_call x1, Pallas kernels, late_correlate(): pl.pallas_call(kernel, grid=(gram_steps + chans // STEP_CHANS,), out_shap...  14.9 us
    pallas_call x2, Pallas kernels, whiten(): pl.pallas_call(whiten_kernel, grid=(chans // WHITEN_CHANS,), out_shape=ja...  14.9 us
    unnamed x20, local copies, waits for them, and re-layouts  11.8 us
    pallas_call x1, Pallas kernels, early_cross(): pl.pallas_call(early_kernel, grid=(steps,), out_shape=jax.ShapeDtypeStruc...  4.4 us
    ppermute x2, starting transfers between devices, neighbours(): near = lax.ppermute(own, 'chan', [(i, i - 1) for i in range(1, count)])  2.7 us
    ppermute x2, starting transfers between devices, relayed(): return lax.ppermute(near, 'chan', [(i, i - 1) for i in range(1, count, 2)])  2.56 us
  transfers between devices with their start and end apart: 6, of which 2 were waited for; matrix products, arithmetic and copies ran while one was open for 0% of the time, Pallas kernels for 17%

profile of v6, /device:TPU:0, one launch (start us, length us, event | category | flops | bytes accessed | tf_op | source)
XLA Modules:
  0.0 71.2 jit_solution(10121878305129981100)
XLA Ops:
  0.0 7.4 %shard_map.83.own_ref = bf16[80,4096]{1,0:T(8,128)(2,1)} custom-call(bf16[80,16,1500]{2,1,0:T(8,128)(2,1)} %traces_ref.3, s32[16,80]{1,0:T(8,128)} %bitcast.2, bf16[1536,512]{1,0:T(8,128)(2,1)} %constant.8.clone.dft_ref, bf16[256,128]{1,0:T(8,128)(2,1)} %constant.9.clone.band_ref), custom_call_target="tpu_custom_call" | custom-call | flops 1966080000 | bytes 8000000 | tf_op jit(solution)/shard_map/pallas_call | solution.py:116
  7.4 0.0 copy-start.7
  7.4 1.4 %collective-permute-start.1 = (bf16[80,4096]{1,0:T(8,128)(2,1)}, bf16[80,4096]{1,0:T(8,128)(2,1)S(1)}, u32[]{:S(2)}, u32[]{:S(2)}) collective-permute-start(bf16[80,4096]{1,0:T(8,128)(2,1)} %shard_map.83.own_ref), channel_id=1, source_target_pairs={{1,0},{2,1},{3,2},{4,3},{5,4},{6,5},{7,6},{8,7},{9,8},{10,9},{11,1... | collective-permute-start | bytes 1966088 | tf_op jit(solution)/shard_map/ppermute | solution.py:307
  8.8 0.7 collective-permute-start.2
  9.5 7.4 %shard_map.82.near_ref.far_ref.refs_1_ = bf16[80,4096]{1,0:T(8,128)(2,1)} custom-call(bf16[80,16,1500]{2,1,0:T(8,128)(2,1)} %traces_ref.3, s32[16,80]{1,0:T(8,128)} %bitcast.3, bf16[1536,512]{1,0:T(8,128)(2,1)} %constant.10.clone.dft_ref, bf16[256,128]{1,0:T(8,128)(2,1)} %constant.9.clone.band_ref), custom_call_target="tpu_custom_call" | custom-call | flops 1966080000 | bytes 8000000 | tf_op jit(solution)/shard_map/pallas_call | solution.py:116
  17.0 0.0 collective-permute-done.1.value_ref
  17.0 0.0 copy-start.5
  17.0 0.9 %copy-done.5 = bf16[80,4096]{1,0:T(8,128)(2,1)} copy-done((bf16[80,4096]{1,0:T(8,128)(2,1)}, bf16[80,4096]{1,0:T(8,128)(2,1)S(1)}, u32[]{:S(2)}) %copy-start.5) | copy-done | bytes 655384
  17.9 1.3 %collective-permute-start.3 = (bf16[80,4096]{1,0:T(8,128)(2,1)}, bf16[80,4096]{1,0:T(8,128)(2,1)S(1)}, u32[]{:S(2)}, u32[]{:S(2)}) collective-permute-start(bf16[80,4096]{1,0:T(8,128)(2,1)} %shard_map.84.near_ref), channel_id=1, source_target_pairs={{1,0},{3,2},{5,4},{7,6},{9,8},{11,10},{13,12},{15,14},{17,16},{19,... | collective-permute-start | bytes 1966088 | tf_op jit(solution)/shard_map/ppermute | solution.py:314
  19.1 0.7 collective-permute-start.4
  19.9 1.3 %collective-permute-start = (bf16[80,4096]{1,0:T(8,128)(2,1)}, bf16[80,4096]{1,0:T(8,128)(2,1)S(1)}, u32[]{:S(2)}, u32[]{:S(2)}) collective-permute-start(bf16[80,4096]{1,0:T(8,128)(2,1)} %shard_map.82.near_ref.far_ref.refs_1_), channel_id=1, source_target_pairs={{1,0},{2,1},{3,2},{4,3},{5,4},{6,5},{7,6},{8,7},{9,8},{10,9},{11,1... | collective-permute-start | bytes 1966088 | tf_op jit(solution)/shard_map/ppermute | solution.py:307
  21.2 0.0 collective-permute-done.2.far_odd_ref
  21.2 8.9 %collective-permute-done.3.far_even_ref = bf16[80,4096]{1,0:T(8,128)(2,1)S(1)} collective-permute-done((bf16[80,4096]{1,0:T(8,128)(2,1)}, bf16[80,4096]{1,0:T(8,128)(2,1)S(1)}, u32[]{:S(2)}, u32[]{:S(2)}) %collective-permute-start.3) | collective-permute-done | bytes 655392 | tf_op jit(solution)/shard_map/ppermute | solution.py:314
  30.1 0.0 copy-done.7
  30.1 0.0 copy-start.6
  30.1 1.1 %copy-done.6 = bf16[80,4096]{1,0:T(8,128)(2,1)S(1)} copy-done((bf16[80,4096]{1,0:T(8,128)(2,1)S(1)}, bf16[80,4096]{1,0:T(8,128)(2,1)}, u32[]{:S(2)}) %copy-start.6) | copy-done | bytes 655384
  31.2 4.4 %shard_map.85.near_ref.far_ref.refs_5_ = bf16[80,256,256]{2,1,0:T(8,128)(2,1)S(1)} custom-call(bf16[80,4096]{1,0:T(8,128)(2,1)S(1)} %copy-done.7, bf16[80,4096]{1,0:T(8,128)(2,1)S(1)} %copy-done.6, bf16[80,4096]{1,0:T(8,128)(2,1)S(1)} %collective-permute-done.2.far_odd_ref, bf16[80,4096]{1,0:T(8,128)(2,1)S(1)} %collective-permute-done.3.far_even_ref), custom_call_target="tpu_custom_call" | custom-call | flops 8000000000 | bytes 13000000 | tf_op jit(solution)/shard_map/pallas_call | solution.py:181
  35.6 0.0 copy-start
  35.6 4.0 %copy-done = bf16[80,256,256]{2,1,0:T(8,128)(2,1)} copy-done((bf16[80,256,256]{2,1,0:T(8,128)(2,1)}, bf16[80,256,256]{2,1,0:T(8,128)(2,1)S(1)}, u32[]{:S(2)}) %copy-start) | copy-done | bytes 10485784
  39.6 0.0 copy-start.2
  39.6 0.0 copy-start.8
  39.6 0.0 copy-start.9
  39.6 0.0 collective-permute-done.value_ref
  39.6 0.0 copy-start.3
  39.6 0.8 %copy-done.3 = bf16[80,4096]{1,0:T(8,128)(2,1)} copy-done((bf16[80,4096]{1,0:T(8,128)(2,1)}, bf16[80,4096]{1,0:T(8,128)(2,1)S(1)}, u32[]{:S(2)}) %copy-start.3) | copy-done | bytes 655384
  40.5 1.3 %collective-permute-start.5 = (bf16[80,4096]{1,0:T(8,128)(2,1)}, bf16[80,4096]{1,0:T(8,128)(2,1)S(1)}, u32[]{:S(2)}, u32[]{:S(2)}) collective-permute-start(bf16[80,4096]{1,0:T(8,128)(2,1)} %shard_map.86.refs_2_), channel_id=1, source_target_pairs={{1,0},{3,2},{5,4},{7,6},{9,8},{11,10},{13,12},{15,14},{17,16},{19,... | collective-permute-start | bytes 1966088 | tf_op jit(solution)/shard_map/ppermute | solution.py:314
  41.7 0.0 collective-permute-done.4.refs_3_
  41.8 9.4 %collective-permute-done.5.refs_4_ = bf16[80,4096]{1,0:T(8,128)(2,1)S(1)} collective-permute-done((bf16[80,4096]{1,0:T(8,128)(2,1)}, bf16[80,4096]{1,0:T(8,128)(2,1)S(1)}, u32[]{:S(2)}, u32[]{:S(2)}) %collective-permute-start.5) | collective-permute-done | bytes 655392 | tf_op jit(solution)/shard_map/ppermute | solution.py:314
  51.2 0.0 copy-done.2
  51.2 0.0 copy-done.8
  51.2 0.0 copy-done.9
  51.2 0.0 copy-start.1
  51.2 4.0 %copy-done.1 = bf16[80,256,256]{2,1,0:T(8,128)(2,1)S(1)} copy-done((bf16[80,256,256]{2,1,0:T(8,128)(2,1)S(1)}, bf16[80,256,256]{2,1,0:T(8,128)(2,1)}, u32[]{:S(2)}) %copy-start.1) | copy-done | bytes 10485784
  55.2 0.0 copy-start.4
  55.2 1.1 %copy-done.4 = bf16[80,4096]{1,0:T(8,128)(2,1)S(1)} copy-done((bf16[80,4096]{1,0:T(8,128)(2,1)S(1)}, bf16[80,4096]{1,0:T(8,128)(2,1)}, u32[]{:S(2)}) %copy-start.4) | copy-done | bytes 655384
  56.3 14.9 %shard_map.87 = bf16[161,80,201]{2,1,0:T(8,128)(2,1)} custom-call(s32[80]{0:T(128)S(1)} %copy-done.8, bf16[80,4096]{1,0:T(8,128)(2,1)S(1)} %copy-done.2, bf16[80,4096]{1,0:T(8,128)(2,1)S(1)} %copy-done.4, bf16[80,4096]{1,0:T(8,128)(2,1)S(1)} %collective-permute-done.4.refs_3_, bf16[80,4096]{1,0:T(8,128)(2,1)S(1)} %collective-permute-done.5.refs_4_, ...), custom_call_target="tpu_custom_call" | custom-call | flops 12000000000 | bytes 20000000 | tf_op jit(solution)/shard_map/pallas_call | solution.py:261
  (2 shorter events, 0.0 us)
Async XLA Ops:
  7.4 22.7 %copy-start.7 = (bf16[80,4096]{1,0:T(8,128)(2,1)S(1)}, bf16[80,4096]{1,0:T(8,128)(2,1)}, u32[]{:S(2)}) copy-start(bf16[80,4096]{1,0:T(8,128)(2,1)} %shard_map.83.own_ref) | copy-start | bytes 1966084
  7.4 9.6 %collective-permute-start.1 = (bf16[80,4096]{1,0:T(8,128)(2,1)}, bf16[80,4096]{1,0:T(8,128)(2,1)S(1)}, u32[]{:S(2)}, u32[]{:S(2)}) collective-permute-start(bf16[80,4096]{1,0:T(8,128)(2,1)} %shard_map.83.own_ref), channel_id=1, source_target_pairs={{1,0},{2,1},{3,2},{4,3},{5,4},{6,5},{7,6},{8,7},{9,8},{10,9},{11,1... | collective-permute-start | bytes 1966088 | tf_op jit(solution)/shard_map/ppermute | solution.py:307
  8.8 12.3 %collective-permute-start.2 = (bf16[80,4096]{1,0:T(8,128)(2,1)}, bf16[80,4096]{1,0:T(8,128)(2,1)S(1)}, u32[]{:S(2)}, u32[]{:S(2)}) collective-permute-start(bf16[80,4096]{1,0:T(8,128)(2,1)} %shard_map.83.own_ref), channel_id=1, source_target_pairs={{3,1},{5,3},{7,5},{9,7},{11,9},{13,11},{15,13},{19,17},{21,19},{23... | collective-permute-start | bytes 1966088 | tf_op jit(solution)/shard_map/ppermute | solution.py:308
  17.0 0.9 %copy-start.5 = (bf16[80,4096]{1,0:T(8,128)(2,1)}, bf16[80,4096]{1,0:T(8,128)(2,1)S(1)}, u32[]{:S(2)}) copy-start(bf16[80,4096]{1,0:T(8,128)(2,1)S(1)} %collective-permute-done.1.value_ref) | copy-start | bytes 1966084
  17.9 12.3 %collective-permute-start.3 = (bf16[80,4096]{1,0:T(8,128)(2,1)}, bf16[80,4096]{1,0:T(8,128)(2,1)S(1)}, u32[]{:S(2)}, u32[]{:S(2)}) collective-permute-start(bf16[80,4096]{1,0:T(8,128)(2,1)} %shard_map.84.near_ref), channel_id=1, source_target_pairs={{1,0},{3,2},{5,4},{7,6},{9,8},{11,10},{13,12},{15,14},{17,16},{19,... | collective-permute-start | bytes 1966088 | tf_op jit(solution)/shard_map/ppermute | solution.py:314
  19.1 22.6 %collective-permute-start.4 = (bf16[80,4096]{1,0:T(8,128)(2,1)}, bf16[80,4096]{1,0:T(8,128)(2,1)S(1)}, u32[]{:S(2)}, u32[]{:S(2)}) collective-permute-start(bf16[80,4096]{1,0:T(8,128)(2,1)} %shard_map.82.near_ref.far_ref.refs_1_), channel_id=1, source_target_pairs={{3,1},{5,3},{7,5},{9,7},{11,9},{13,11},{15,13},{19,17},{21,19},{23... | collective-permute-start | bytes 1966088 | tf_op jit(solution)/shard_map/ppermute | solution.py:308
  19.9 19.8 %collective-permute-start = (bf16[80,4096]{1,0:T(8,128)(2,1)}, bf16[80,4096]{1,0:T(8,128)(2,1)S(1)}, u32[]{:S(2)}, u32[]{:S(2)}) collective-permute-start(bf16[80,4096]{1,0:T(8,128)(2,1)} %shard_map.82.near_ref.far_ref.refs_1_), channel_id=1, source_target_pairs={{1,0},{2,1},{3,2},{4,3},{5,4},{6,5},{7,6},{8,7},{9,8},{10,9},{11,1... | collective-permute-start | bytes 1966088 | tf_op jit(solution)/shard_map/ppermute | solution.py:307
  30.1 1.1 %copy-start.6 = (bf16[80,4096]{1,0:T(8,128)(2,1)S(1)}, bf16[80,4096]{1,0:T(8,128)(2,1)}, u32[]{:S(2)}) copy-start(bf16[80,4096]{1,0:T(8,128)(2,1)} %shard_map.84.near_ref) | copy-start | bytes 1966084
  35.6 4.0 %copy-start = (bf16[80,256,256]{2,1,0:T(8,128)(2,1)}, bf16[80,256,256]{2,1,0:T(8,128)(2,1)S(1)}, u32[]{:S(2)}) copy-start(bf16[80,256,256]{2,1,0:T(8,128)(2,1)S(1)} %shard_map.85.near_ref.far_ref.refs_5_) | copy-start | bytes 31457284
  39.6 11.6 %copy-start.2 = (bf16[80,4096]{1,0:T(8,128)(2,1)S(1)}, bf16[80,4096]{1,0:T(8,128)(2,1)}, u32[]{:S(2)}) copy-start(bf16[80,4096]{1,0:T(8,128)(2,1)} %shard_map.82.near_ref.far_ref.refs_1_) | copy-start | bytes 1966084
  39.6 11.6 %copy-start.8 = (s32[80]{0:T(128)S(1)}, s32[80]{0:T(128)}, u32[]{:S(2)}) copy-start(s32[80]{0:T(128)} %refs_0_.1) | copy-start | bytes 964
  39.6 11.6 %copy-start.9 = (bf16[208,512]{1,0:T(8,128)(2,1)S(1)}, bf16[208,512]{1,0:T(8,128)(2,1)}, u32[]{:S(2)}) copy-start(bf16[208,512]{1,0:T(8,128)(2,1)} %constant.11.clone.refs_6_) | copy-start | bytes 638980
  39.6 0.8 %copy-start.3 = (bf16[80,4096]{1,0:T(8,128)(2,1)}, bf16[80,4096]{1,0:T(8,128)(2,1)S(1)}, u32[]{:S(2)}) copy-start(bf16[80,4096]{1,0:T(8,128)(2,1)S(1)} %collective-permute-done.value_ref) | copy-start | bytes 1966084
  40.5 10.7 %collective-permute-start.5 = (bf16[80,4096]{1,0:T(8,128)(2,1)}, bf16[80,4096]{1,0:T(8,128)(2,1)S(1)}, u32[]{:S(2)}, u32[]{:S(2)}) collective-permute-start(bf16[80,4096]{1,0:T(8,128)(2,1)} %shard_map.86.refs_2_), channel_id=1, source_target_pairs={{1,0},{3,2},{5,4},{7,6},{9,8},{11,10},{13,12},{15,14},{17,16},{19,... | collective-permute-start | bytes 1966088 | tf_op jit(solution)/shard_map/ppermute | solution.py:314
  51.2 4.0 %copy-start.1 = (bf16[80,256,256]{2,1,0:T(8,128)(2,1)S(1)}, bf16[80,256,256]{2,1,0:T(8,128)(2,1)}, u32[]{:S(2)}) copy-start(bf16[80,256,256]{2,1,0:T(8,128)(2,1)} %copy-done) | copy-start | bytes 31457284
  55.2 1.1 %copy-start.4 = (bf16[80,4096]{1,0:T(8,128)(2,1)S(1)}, bf16[80,4096]{1,0:T(8,128)(2,1)}, u32[]{:S(2)}) copy-start(bf16[80,4096]{1,0:T(8,128)(2,1)} %shard_map.86.refs_2_) | copy-start | bytes 1966084
